TPU v7x, 128 devices: a whole 4x4x4 slice. The times are simulated.
128 devices in a mesh: gr: 16 (over y_lo, z, core), gc: 8 (over x, y_hi).
Axes of the slice: x: 4, y: 4 (y_hi: 2, y_lo: 2; y = y_hi * 2 + y_lo), z: 4, core: 2. Of those that a mesh axis runs over, the one named last changes fastest.
Arguments:
- features: bfloat16 [65536, 256], P(('gr', 'gc')), may hold values from -6 to 6
- block_values: bfloat16 [16, 8, 384, 128, 128], P('gr', 'gc')
- block_row: int32 [16, 8, 384], P('gr', 'gc'), may hold values from 0 to 31
- block_col: int32 [16, 8, 384], P('gr', 'gc'), may hold values from 0 to 63
- block_count: int32 [16, 8], P('gr', 'gc'), may hold values from 96 to 384, as said below
- weight_self: bfloat16 [256, 256], replicated, may hold values from -0.375 to 0.375
- weight_neigh: bfloat16 [256, 256], replicated, may hold values from -0.375 to 0.375
- bias: float32 [256], replicated, may hold values from -0.5 to 0.5
- cotangent: bfloat16 [65536, 256], P(('gr', 'gc')), may hold values from -6 to 6
Outputs:
- activations: bfloat16 [65536, 256], P(('gr', 'gc'))
- grad_features: bfloat16 [65536, 256], P(('gr', 'gc'))
- grad_self: float32 [256, 256], replicated
- grad_neigh: float32 [256, 256], replicated
- grad_bias: float32 [256], replicated
Inputs may be any that keep to these rules, and one draw needn't show every extreme that they name: Slots 0 to block_count - 1 of a grid cell are live; some grid cell holds exactly 384 live slots.
All inputs are finite; a program needn't handle non-finite values.
Results may differ from a plain program's by a relative error of at most 0.007.
Values may be sent and summed in bfloat16 or wider, within the bound.
A program may use at most 128 MiB of HBM per device.

v0:
```python
import math

import jax
import jax.numpy as jnp
from jax import lax
from jax.sharding import PartitionSpec as P


def block_pass(tiles, take_index, put_index, live, source, out_blocks, transpose):
    slots = tiles.shape[0]
    group = math.gcd(slots, 64)
    width = source.shape[1]
    source_tiles = source.reshape(-1, 128, width)
    in_blocks = source_tiles.shape[0]
    take_range = jnp.arange(in_blocks, dtype=jnp.int32)
    put_range = jnp.arange(out_blocks, dtype=jnp.int32)
    form = "gji,gjf->gif" if transpose else "gij,gjf->gif"

    def step(turn, total):
        begin = turn * group
        tile_group = lax.dynamic_slice_in_dim(tiles, begin, group, 0)
        take_group = lax.dynamic_slice_in_dim(take_index, begin, group, 0)
        put_group = lax.dynamic_slice_in_dim(put_index, begin, group, 0)
        keep_group = lax.dynamic_slice_in_dim(live, begin, group, 0)
        take_onehot = (take_group[:, None] == take_range[None, :]).astype(jnp.bfloat16)
        picked = jnp.einsum(
            "gb,bjf->gjf", take_onehot, source_tiles, preferred_element_type=jnp.float32
        ).astype(jnp.bfloat16)
        prods = jnp.einsum(form, tile_group, picked, preferred_element_type=jnp.float32)
        put_onehot = (put_group[:, None] == put_range[None, :]).astype(jnp.float32) * keep_group[
            :, None
        ]
        added = jnp.einsum(
            "gb,gif->bif",
            put_onehot,
            prods,
            precision=lax.Precision.HIGHEST,
            preferred_element_type=jnp.float32,
        )
        return total + added

    total = jnp.zeros((out_blocks, 128, width), jnp.float32)
    total = lax.fori_loop(0, slots // group, step, total)
    return total.reshape(out_blocks * 128, width)


def tile_degrees(tiles, put_index, live, out_blocks):
    nonzero = jnp.sum((tiles != 0).astype(jnp.float32), axis=2)
    put_range = jnp.arange(out_blocks, dtype=jnp.int32)
    put_onehot = (put_index[:, None] == put_range[None, :]).astype(jnp.float32) * live[:, None]
    total = jnp.einsum(
        "sb,si->bi",
        put_onehot,
        nonzero,
        precision=lax.Precision.HIGHEST,
        preferred_element_type=jnp.float32,
    )
    return total.reshape(-1)


def dense_forward(own_feats, neigh_mean, weight_self, weight_neigh, bias, own_cot, counts):
    preact = (
        jnp.dot(own_feats, weight_self, preferred_element_type=jnp.float32)
        + jnp.dot(neigh_mean, weight_neigh, preferred_element_type=jnp.float32)
        + bias[None, :]
    )
    sigma = jax.nn.sigmoid(preact)
    activations = (preact * sigma).astype(jnp.bfloat16)
    grad_pre = (own_cot.astype(jnp.float32) * sigma * (1.0 + preact * (1.0 - sigma))).astype(
        jnp.bfloat16
    )
    projected = lax.dot_general(
        grad_pre, weight_neigh, (((1,), (1,)), ((), ())), preferred_element_type=jnp.float32
    )
    back_rows = (projected / counts).astype(jnp.bfloat16)
    return (activations, grad_pre, back_rows)


def local(
    features,
    block_values,
    block_row,
    block_col,
    block_count,
    weight_self,
    weight_neigh,
    bias,
    cotangent,
):
    rows_here = features.shape[0]
    grid_rows = lax.axis_size("gr")
    grid_cols = lax.axis_size("gc")
    nodes_total = rows_here * grid_rows * grid_cols
    tiles = block_values.reshape(block_values.shape[2], 128, 128)
    tile_rows = block_row.reshape(-1)
    tile_cols = block_col.reshape(-1)
    live = (jnp.arange(tiles.shape[0], dtype=jnp.int32) < block_count.reshape(())).astype(
        jnp.float32
    )
    row_blocks = rows_here * grid_cols // 128
    col_blocks = rows_here * grid_rows // 128
    column_feats = lax.all_gather(features, "gr", axis=0, tiled=True)
    partial_rows = block_pass(tiles, tile_cols, tile_rows, live, column_feats, row_blocks, False)
    partial_degree = tile_degrees(tiles, tile_rows, live, row_blocks)
    summed, degree = (
        lax.psum_scatter(partial_rows, "gc", scatter_dimension=0, tiled=True),
        lax.psum_scatter(partial_degree, "gc", scatter_dimension=0, tiled=True),
    )
    counts = jnp.maximum(degree, 1.0)[:, None]
    neigh_mean = (summed / counts).astype(jnp.bfloat16)
    activations, grad_pre, back_rows = dense_forward(
        features, neigh_mean, weight_self, weight_neigh, bias, cotangent, counts
    )
    row_back = lax.all_gather(back_rows, "gc", axis=0, tiled=True)
    scale = 1.0 / math.sqrt(nodes_total)
    contract_rows = (((0,), (0,)), ((), ()))
    local_self = lax.dot_general(
        features, grad_pre, contract_rows, preferred_element_type=jnp.float32
    )
    local_bias = jnp.sum(grad_pre.astype(jnp.float32), axis=0)
    partial_cols = block_pass(tiles, tile_rows, tile_cols, live, row_back, col_blocks, True)
    back_sum = lax.psum_scatter(partial_cols, "gr", scatter_dimension=0, tiled=True)
    direct = lax.dot_general(
        grad_pre, weight_self, (((1,), (1,)), ((), ())), preferred_element_type=jnp.float32
    )
    grad_features = (direct + back_sum).astype(jnp.bfloat16)
    local_neigh = lax.dot_general(
        neigh_mean, grad_pre, contract_rows, preferred_element_type=jnp.float32
    )
    sum_self, sum_neigh, sum_bias = lax.psum((local_self, local_neigh, local_bias), ("gr", "gc"))
    return (activations, grad_features, sum_self * scale, sum_neigh * scale, sum_bias * scale)


def solution(mesh):
    placed = (
        P(("gr", "gc"), None),
        P("gr", "gc", None, None, None),
        P("gr", "gc", None),
        P("gr", "gc", None),
        P("gr", "gc"),
        P(),
        P(),
        P(),
        P(("gr", "gc"), None),
    )
    return jax.shard_map(
        local,
        mesh=mesh,
        in_specs=placed,
        out_specs=(P(("gr", "gc"), None), P(("gr", "gc"), None), P(), P(), P()),
        check_vma=False,
    )
```

profile of v0, /device:TPU:0, one launch (start us, length us, event | category | flops | bytes accessed | tf_op | source)
XLA Modules:
  0.0 625.2 jit_solution(1976260389418445021)
XLA Ops:
  10.0 39.6 %all-gather.3.cloned.1.call-done = bf16[8192,256]{1,0:T(8,128)(2,1)} async-done(((bf16[512,256]{1,0:T(8,128)(2,1)}), bf16[8192,256]{1,0:T(8,128)(2,1)}) %all-gather.3.cloned.1.call-update) | async-done | bytes 4194320 | tf_op jit(solution)/shard_map/all_gather | solution.py:102
  49.7 183.9 %while.28 = (s32[]{:T(128)}, f32[32,128,256]{2,0,1:T(8,128)}, s32[384]{0:T(512)S(1)}, f32[384]{0:T(512)S(1)}, bf16[384,128,128]{2,1,0:T(8,128)(2,1)}, /*index=5*...) while((s32[]{:T(128)}, f32[32,128,256]{2,0,1:T(8,128)}, ...), condition=%wide.region_1.0_spmd.clone, body=%wide.region_0.0_spmd.clone.sunk | while | flops 1612718080 | bytes 39848380 | solution.py:43
  49.7 5.5 fusion.87
  55.2 7.8 %fusion.88 = f32[64,128,256]{2,1,0:T(8,128)} fusion(bf16[64,128,256]{2,0,1:T(8,128)(2,1)S(1)} %fusion.87, bf16[384,128,128]{2,1,0:T(8,128)(2,1)} %get-tuple-element.528, s32[]{:T(128)S(6)} %select_n.24), kind=kOutput, calls=%fused_computation.7.clone.1 | convolution fusion | flops 536870912 | bytes 14680068 | tf_op jit(solution)/shard_map/while/body/eval_jaxpr/gij,gjf->gif/dot_general | solution.py:29
  63.2 14.1 %select_add_fusion.4 = f32[32,128,256]{2,0,1:T(8,128)} fusion(f32[32,128,256]{2,0,1:T(8,128)} %get-tuple-element.514, f32[64,128,256]{2,1,0:T(8,128)} %fusion.88, pred[]{:T(512)S(6)} %compare.6, f32[64]{0:T(128)S(1)} %dynamic_slice.78, s32[64]{0:T(128)S(1)} %dynamic_slice.79), kind=kOutput, calls=%fused_computation.10.clone.1 | convolution fusion | flops 807407616 | bytes 16777728 | tf_op jit(solution)/shard_map/while/body/eval_jaxpr/gb,gif->bif/dot_general | solution.py:33
  77.4 5.5 fusion.87
  82.8 7.8 %fusion.88 = f32[64,128,256]{2,1,0:T(8,128)} fusion(bf16[64,128,256]{2,0,1:T(8,128)(2,1)S(1)} %fusion.87, bf16[384,128,128]{2,1,0:T(8,128)(2,1)} %get-tuple-element.528, s32[]{:T(128)S(6)} %select_n.24), kind=kOutput, calls=%fused_computation.7.clone.1 | convolution fusion | flops 536870912 | bytes 14680068 | tf_op jit(solution)/shard_map/while/body/eval_jaxpr/gij,gjf->gif/dot_general | solution.py:29
  90.8 14.8 %select_add_fusion.4 = f32[32,128,256]{2,0,1:T(8,128)} fusion(f32[32,128,256]{2,0,1:T(8,128)} %get-tuple-element.514, f32[64,128,256]{2,1,0:T(8,128)} %fusion.88, pred[]{:T(512)S(6)} %compare.6, f32[64]{0:T(128)S(1)} %dynamic_slice.78, s32[64]{0:T(128)S(1)} %dynamic_slice.79), kind=kOutput, calls=%fused_computation.10.clone.1 | convolution fusion | flops 807407616 | bytes 16777728 | tf_op jit(solution)/shard_map/while/body/eval_jaxpr/gb,gif->bif/dot_general | solution.py:33
  105.7 5.5 fusion.87
  111.1 7.8 %fusion.88 = f32[64,128,256]{2,1,0:T(8,128)} fusion(bf16[64,128,256]{2,0,1:T(8,128)(2,1)S(1)} %fusion.87, bf16[384,128,128]{2,1,0:T(8,128)(2,1)} %get-tuple-element.528, s32[]{:T(128)S(6)} %select_n.24), kind=kOutput, calls=%fused_computation.7.clone.1 | convolution fusion | flops 536870912 | bytes 14680068 | tf_op jit(solution)/shard_map/while/body/eval_jaxpr/gij,gjf->gif/dot_general | solution.py:29
  119.1 14.8 %select_add_fusion.4 = f32[32,128,256]{2,0,1:T(8,128)} fusion(f32[32,128,256]{2,0,1:T(8,128)} %get-tuple-element.514, f32[64,128,256]{2,1,0:T(8,128)} %fusion.88, pred[]{:T(512)S(6)} %compare.6, f32[64]{0:T(128)S(1)} %dynamic_slice.78, s32[64]{0:T(128)S(1)} %dynamic_slice.79), kind=kOutput, calls=%fused_computation.10.clone.1 | convolution fusion | flops 807407616 | bytes 16777728 | tf_op jit(solution)/shard_map/while/body/eval_jaxpr/gb,gif->bif/dot_general | solution.py:33
  139.4 7.8 %fusion.88 = f32[64,128,256]{2,1,0:T(8,128)} fusion(bf16[64,128,256]{2,0,1:T(8,128)(2,1)S(1)} %fusion.87, bf16[384,128,128]{2,1,0:T(8,128)(2,1)} %get-tuple-element.528, s32[]{:T(128)S(6)} %select_n.24), kind=kOutput, calls=%fused_computation.7.clone.1 | convolution fusion | flops 536870912 | bytes 14680068 | tf_op jit(solution)/shard_map/while/body/eval_jaxpr/gij,gjf->gif/dot_general | solution.py:29
  147.4 14.8 %select_add_fusion.4 = f32[32,128,256]{2,0,1:T(8,128)} fusion(f32[32,128,256]{2,0,1:T(8,128)} %get-tuple-element.514, f32[64,128,256]{2,1,0:T(8,128)} %fusion.88, pred[]{:T(512)S(6)} %compare.6, f32[64]{0:T(128)S(1)} %dynamic_slice.78, s32[64]{0:T(128)S(1)} %dynamic_slice.79), kind=kOutput, calls=%fused_computation.10.clone.1 | convolution fusion | flops 807407616 | bytes 16777728 | tf_op jit(solution)/shard_map/while/body/eval_jaxpr/gb,gif->bif/dot_general | solution.py:33
  167.7 7.8 %fusion.88 = f32[64,128,256]{2,1,0:T(8,128)} fusion(bf16[64,128,256]{2,0,1:T(8,128)(2,1)S(1)} %fusion.87, bf16[384,128,128]{2,1,0:T(8,128)(2,1)} %get-tuple-element.528, s32[]{:T(128)S(6)} %select_n.24), kind=kOutput, calls=%fused_computation.7.clone.1 | convolution fusion | flops 536870912 | bytes 14680068 | tf_op jit(solution)/shard_map/while/body/eval_jaxpr/gij,gjf->gif/dot_general | solution.py:29
  175.7 14.8 %select_add_fusion.4 = f32[32,128,256]{2,0,1:T(8,128)} fusion(f32[32,128,256]{2,0,1:T(8,128)} %get-tuple-element.514, f32[64,128,256]{2,1,0:T(8,128)} %fusion.88, pred[]{:T(512)S(6)} %compare.6, f32[64]{0:T(128)S(1)} %dynamic_slice.78, s32[64]{0:T(128)S(1)} %dynamic_slice.79), kind=kOutput, calls=%fused_computation.10.clone.1 | convolution fusion | flops 807407616 | bytes 16777728 | tf_op jit(solution)/shard_map/while/body/eval_jaxpr/gb,gif->bif/dot_general | solution.py:33
  190.5 5.5 fusion.87
  196.0 7.8 %fusion.88 = f32[64,128,256]{2,1,0:T(8,128)} fusion(bf16[64,128,256]{2,0,1:T(8,128)(2,1)S(1)} %fusion.87, bf16[384,128,128]{2,1,0:T(8,128)(2,1)} %get-tuple-element.528, s32[]{:T(128)S(6)} %select_n.24), kind=kOutput, calls=%fused_computation.7.clone.1 | convolution fusion | flops 536870912 | bytes 14680068 | tf_op jit(solution)/shard_map/while/body/eval_jaxpr/gij,gjf->gif/dot_general | solution.py:29
  204.0 14.8 %select_add_fusion.4 = f32[32,128,256]{2,0,1:T(8,128)} fusion(f32[32,128,256]{2,0,1:T(8,128)} %get-tuple-element.514, f32[64,128,256]{2,1,0:T(8,128)} %fusion.88, pred[]{:T(512)S(6)} %compare.6, f32[64]{0:T(128)S(1)} %dynamic_slice.78, s32[64]{0:T(128)S(1)} %dynamic_slice.79), kind=kOutput, calls=%fused_computation.10.clone.1 | convolution fusion | flops 807407616 | bytes 16777728 | tf_op jit(solution)/shard_map/while/body/eval_jaxpr/gb,gif->bif/dot_general | solution.py:33
  233.6 6.6 %copy.19 = f32[32,128,256]{2,1,0:T(8,128)} copy(f32[32,128,256]{2,0,1:T(8,128)} %get-tuple-element.313) | data formatting | bytes 8388608 | tf_op jit(solution)/shard_map/while | solution.py:43
  242.1 8.0 %convert_reduce_fusion = f32[384,128]{1,0:T(8,128)S(1)} fusion(bf16[1,1,384,128,128]{4,3,2,1,0:T(8,128)(2,1)} %bitcast.50), kind=kLoop, calls=%fused_computation.42 | loop fusion | flops 18825216 | bytes 12779520 | tf_op jit(solution)/shard_map/reduce_sum | solution.py:48
  250.7 42.0 %all-reduce = f32[4096]{0:T(1024)S(1)} all-reduce(f32[4096]{0:T(1024)S(1)} %convolution_bitcast_fusion.1), channel_id=3, replica_groups=mesh['gr'=16,'gc'=8] {'gc'}, use_global_device_ids=true, to_apply=%region_4.0.clone | all-reduce | flops 4096 | bytes 32768
  293.1 32.1 %reduce-scatter.3.cloned.1.call-done = f32[512,256]{1,0:T(8,128)} async-done(((f32[4096,256]{1,0:T(8,128)}), f32[512,256]{1,0:T(8,128)}) %reduce-scatter.3.cloned.1.call-update) | async-done | bytes 524304 | tf_op jit(solution)/shard_map/reduce_scatter | solution.py:106
  330.6 51.8 %all-gather.5.cloned.1.call-done = bf16[4096,256]{1,0:T(8,128)(2,1)} async-done(((bf16[512,256]{1,0:T(8,128)(2,1)}), bf16[4096,256]{1,0:T(8,128)(2,1)}) %all-gather.5.cloned.1.call-update) | async-done | bytes 2097168 | tf_op jit(solution)/shard_map/all_gather | solution.py:114
  382.4 147.6 %while.29 = (s32[]{:T(128)}, f32[64,128,256]{2,0,1:T(8,128)}, s32[384]{0:T(512)S(1)}, f32[384]{0:T(512)S(1)}, bf16[384,128,128]{2,1,0:T(8,128)(2,1)}, /*index=5*...) while((s32[]{:T(128)}, f32[64,128,256]{2,0,1:T(8,128)}, ...), condition=%wide.region_6.0_spmd.clone, body=%wide.region_5.0_spmd.clone.sunk | while | flops 2285905920 | bytes 104860168 | solution.py:43
  391.0 12.8 %select_add_fusion.5 = f32[64,128,256]{2,0,1:T(8,128)S(1)} fusion(f32[64,128,256]{2,0,1:T(8,128)S(1)} %bitcast.47, pred[]{:T(512)S(6)} %compare.7, f32[64,128,256]{2,1,0:T(8,128)S(1)} %fusion.95, f32[64]{0:T(128)S(1)} %dynamic_slice.82, s32[64]{0:T(128)S(1)} %dynamic_slice.83), kind=kOutput, calls=%fused_computation.26.clone.1 | convolution fusion | flops 1614815232 | bytes 25166336 | tf_op jit(solution)/shard_map/while/body/eval_jaxpr/gb,gif->bif/dot_general | solution.py:33
  415.6 12.8 %select_add_fusion.5 = f32[64,128,256]{2,0,1:T(8,128)S(1)} fusion(f32[64,128,256]{2,0,1:T(8,128)S(1)} %bitcast.47, pred[]{:T(512)S(6)} %compare.7, f32[64,128,256]{2,1,0:T(8,128)S(1)} %fusion.95, f32[64]{0:T(128)S(1)} %dynamic_slice.82, s32[64]{0:T(128)S(1)} %dynamic_slice.83), kind=kOutput, calls=%fused_computation.26.clone.1 | convolution fusion | flops 1614815232 | bytes 25166336 | tf_op jit(solution)/shard_map/while/body/eval_jaxpr/gb,gif->bif/dot_general | solution.py:33
  440.2 12.8 %select_add_fusion.5 = f32[64,128,256]{2,0,1:T(8,128)S(1)} fusion(f32[64,128,256]{2,0,1:T(8,128)S(1)} %bitcast.47, pred[]{:T(512)S(6)} %compare.7, f32[64,128,256]{2,1,0:T(8,128)S(1)} %fusion.95, f32[64]{0:T(128)S(1)} %dynamic_slice.82, s32[64]{0:T(128)S(1)} %dynamic_slice.83), kind=kOutput, calls=%fused_computation.26.clone.1 | convolution fusion | flops 1614815232 | bytes 25166336 | tf_op jit(solution)/shard_map/while/body/eval_jaxpr/gb,gif->bif/dot_general | solution.py:33
  464.8 12.8 %select_add_fusion.5 = f32[64,128,256]{2,0,1:T(8,128)S(1)} fusion(f32[64,128,256]{2,0,1:T(8,128)S(1)} %bitcast.47, pred[]{:T(512)S(6)} %compare.7, f32[64,128,256]{2,1,0:T(8,128)S(1)} %fusion.95, f32[64]{0:T(128)S(1)} %dynamic_slice.82, s32[64]{0:T(128)S(1)} %dynamic_slice.83), kind=kOutput, calls=%fused_computation.26.clone.1 | convolution fusion | flops 1614815232 | bytes 25166336 | tf_op jit(solution)/shard_map/while/body/eval_jaxpr/gb,gif->bif/dot_general | solution.py:33
  489.4 12.8 %select_add_fusion.5 = f32[64,128,256]{2,0,1:T(8,128)S(1)} fusion(f32[64,128,256]{2,0,1:T(8,128)S(1)} %bitcast.47, pred[]{:T(512)S(6)} %compare.7, f32[64,128,256]{2,1,0:T(8,128)S(1)} %fusion.95, f32[64]{0:T(128)S(1)} %dynamic_slice.82, s32[64]{0:T(128)S(1)} %dynamic_slice.83), kind=kOutput, calls=%fused_computation.26.clone.1 | convolution fusion | flops 1614815232 | bytes 25166336 | tf_op jit(solution)/shard_map/while/body/eval_jaxpr/gb,gif->bif/dot_general | solution.py:33
  514.0 12.8 %select_add_fusion.5 = f32[64,128,256]{2,0,1:T(8,128)S(1)} fusion(f32[64,128,256]{2,0,1:T(8,128)S(1)} %bitcast.47, pred[]{:T(512)S(6)} %compare.7, f32[64,128,256]{2,1,0:T(8,128)S(1)} %fusion.95, f32[64]{0:T(128)S(1)} %dynamic_slice.82, s32[64]{0:T(128)S(1)} %dynamic_slice.83), kind=kOutput, calls=%fused_computation.26.clone.1 | convolution fusion | flops 1614815232 | bytes 25166336 | tf_op jit(solution)/shard_map/while/body/eval_jaxpr/gb,gif->bif/dot_general | solution.py:33
  530.0 11.5 %copy.20 = f32[64,128,256]{2,1,0:T(8,128)} copy(f32[64,128,256]{2,0,1:T(8,128)} %get-tuple-element.314) | data formatting | bytes 16777216 | tf_op jit(solution)/shard_map/while | solution.py:43
  541.5 70.4 %psum.23 = f32[256]{0:T(256)S(1)} all-reduce(f32[256]{0:T(256)S(1)} %get-tuple-element.411), channel_id=1, replica_groups=mesh['gr'=16,'gc'=8] {'gr','gc'}, use_global_device_ids=true, to_apply=%region_11.0 | all-reduce | flops 256 | bytes 2048 | tf_op jit(solution)/shard_map/psum | solution.py:130
  (137 shorter events, 99.0 us)
Async XLA Ops:
  7.2 319.2 %copy-start = (bf16[256,256]{1,0:T(8,128)(2,1)S(1)}, bf16[256,256]{1,0:T(8,128)(2,1)}, u32[]{:S(2)}) copy-start(bf16[256,256]{1,0:T(8,128)(2,1)} %param.19) | copy-start | bytes 393220
  7.2 42.5 %all-gather.3.cloned.1.call-start = ((), (), s32[]{:S(2)}) async-start(), calls=%async_computation.2 | async-start | bytes 4456448 | tf_op jit(solution)/shard_map/all_gather | solution.py:102
  7.9 317.3 %reduce-scatter.3.cloned.1.call-start = ((), (), s32[]{:S(2)}) async-start(), calls=%async_computation.3 | async-start | bytes 4718592 | tf_op jit(solution)/shard_map/reduce_scatter | solution.py:106
  240.1 0.7 copy-start.7
  240.2 142.3 %all-gather.5.cloned.1.call-start = ((), (), s32[]{:S(2)}) async-start(), calls=%async_computation.4 | async-start | bytes 2359296 | tf_op jit(solution)/shard_map/all_gather | solution.py:114
  242.0 50.8 %copy-start.3 = (bf16[512,256]{1,0:T(8,128)(2,1)S(1)}, bf16[512,256]{1,0:T(8,128)(2,1)}, u32[]{:S(2)}) copy-start(bf16[512,256]{1,0:T(8,128)(2,1)} %param.13) | copy-start | bytes 786436
  242.0 50.8 %copy-start.4 = (bf16[256,256]{1,0:T(8,128)(2,1)S(1)}, bf16[256,256]{1,0:T(8,128)(2,1)}, u32[]{:S(2)}) copy-start(bf16[256,256]{1,0:T(8,128)(2,1)} %param.18) | copy-start | bytes 393220
  242.1 84.3 %copy-start.5 = (bf16[512,256]{1,0:T(8,128)(2,1)S(1)}, bf16[512,256]{1,0:T(8,128)(2,1)}, u32[]{:S(2)}) copy-start(bf16[512,256]{1,0:T(8,128)(2,1)} %param.21) | copy-start | bytes 786436
  242.1 84.3 %copy-start.6 = (f32[256]{0:T(256)S(1)}, f32[256]{0:T(256)}, u32[]{:S(2)}) copy-start(f32[256]{0:T(256)} %param.20) | copy-start | bytes 3076
  328.5 283.9 %all-reduce.4.cloned.1.call-start = ((), (), s32[]{:S(2)}) async-start(), calls=%async_computation.6 | async-start | bytes 1048576 | tf_op jit(solution)/shard_map/psum | solution.py:130
  330.6 285.7 %reduce-scatter.5.cloned.1.call-start = ((), (), s32[]{:S(2)}) async-start(), calls=%async_computation.5 | async-start | bytes 8912896 | tf_op jit(solution)/shard_map/reduce_scatter | solution.py:122
  382.5 8.5 %slice-start = ((s8[8388608]{0:T(1024)(128)(4,1)}), s8[4194304]{0:T(1024)(128)(4,1)S(1)}, s32[]{:S(2)}) async-start(s8[8388608]{0:T(1024)(128)(4,1)} %bitcast.46), calls=%async_computation.7 | async-start | bytes 8388608 | tf_op jit(solution)/shard_map/while
  385.7 5.3 slice-start.1
  403.8 3.2 copy-start.2
  407.1 8.5 %slice-start = ((s8[8388608]{0:T(1024)(128)(4,1)}), s8[4194304]{0:T(1024)(128)(4,1)S(1)}, s32[]{:S(2)}) async-start(s8[8388608]{0:T(1024)(128)(4,1)} %bitcast.46), calls=%async_computation.7 | async-start | bytes 8388608 | tf_op jit(solution)/shard_map/while
  410.4 5.3 slice-start.1
  428.4 3.2 copy-start.2
  431.7 8.5 %slice-start = ((s8[8388608]{0:T(1024)(128)(4,1)}), s8[4194304]{0:T(1024)(128)(4,1)S(1)}, s32[]{:S(2)}) async-start(s8[8388608]{0:T(1024)(128)(4,1)} %bitcast.46), calls=%async_computation.7 | async-start | bytes 8388608 | tf_op jit(solution)/shard_map/while
  435.0 5.2 slice-start.1
  453.0 3.2 copy-start.2
  456.3 8.5 %slice-start = ((s8[8388608]{0:T(1024)(128)(4,1)}), s8[4194304]{0:T(1024)(128)(4,1)S(1)}, s32[]{:S(2)}) async-start(s8[8388608]{0:T(1024)(128)(4,1)} %bitcast.46), calls=%async_computation.7 | async-start | bytes 8388608 | tf_op jit(solution)/shard_map/while
  459.6 5.3 slice-start.1
  477.6 3.2 copy-start.2
  480.9 8.5 %slice-start = ((s8[8388608]{0:T(1024)(128)(4,1)}), s8[4194304]{0:T(1024)(128)(4,1)S(1)}, s32[]{:S(2)}) async-start(s8[8388608]{0:T(1024)(128)(4,1)} %bitcast.46), calls=%async_computation.7 | async-start | bytes 8388608 | tf_op jit(solution)/shard_map/while
  484.2 5.3 slice-start.1
  502.2 3.2 copy-start.2
  505.5 8.5 %slice-start = ((s8[8388608]{0:T(1024)(128)(4,1)}), s8[4194304]{0:T(1024)(128)(4,1)S(1)}, s32[]{:S(2)}) async-start(s8[8388608]{0:T(1024)(128)(4,1)} %bitcast.46), calls=%async_computation.7 | async-start | bytes 8388608 | tf_op jit(solution)/shard_map/while
  508.8 5.3 slice-start.1
  526.8 3.2 copy-start.2
  541.5 76.7 %copy-start.1 = (bf16[256,256]{1,0:T(8,128)(2,1)S(1)}, bf16[256,256]{1,0:T(8,128)(2,1)}, u32[]{:S(2)}) copy-start(bf16[256,256]{1,0:T(8,128)(2,1)} %param.19) | copy-start | bytes 393220
Sparse Core Ops, SparseCore 0:
  9.7 39.8 all-gather.2
  240.3 84.8 reduce-scatter.2
  328.7 53.7 all-gather.4
  387.8 143.7 all-reduce.3
  541.7 74.5 reduce-scatter.4
where the time goes:
time: 634 us; the launch traced here: 625 us
  matrix products  301 us (47%)
  waiting for transfers between devices  125 us (20%)
  blocking collectives  112 us (18%)
  local copies, waits for them, and re-layouts  42.9 us (7%)
  between operations  15.6 us (2%)
  loops' own time  15.1 us (2%)
  other arithmetic  12.4 us (2%)
    dot_general x12, matrix products, step(): jnp.einsum('gb,gif->bif', put_onehot, prods, precision=lax.Precision.HIGH...  165 us
    dot_general x12, matrix products, step(): jnp.einsum(form, tile_group, picked, preferred_element_type=jnp.float32)  77.3 us
    psum x1, blocking collectives, local(): lax.psum((local_self, local_neigh, local_bias), ('gr', 'gc'))  70.4 us
    dot_general x12, matrix products, step(): jnp.einsum('gb,bjf->gjf', take_onehot, source_tiles, preferred_element_ty...  52.3 us
    all_gather x1, waiting for transfers between devices, local(): row_back = lax.all_gather(back_rows, 'gc', axis=0, tiled=True)  51.8 us
    unnamed x1, blocking collectives  42 us
    all_gather x1, waiting for transfers between devices, local(): column_feats = lax.all_gather(features, 'gr', axis=0, tiled=True)  39.6 us
    reduce_scatter x1, waiting for transfers between devices, local(): lax.psum_scatter(partial_rows, 'gc', scatter_dimension=0, tiled=True)  32.1 us
  transfers between devices with their start and end apart: 5, of which 4 were waited for; matrix products, arithmetic and copies ran while one was open for 25% of the time, Pallas kernels for 0%

commit v1 on v0

v1 whole, which is shorter than its diff:
```python
import functools

import jax
import jax.numpy as jnp
from jax import lax
from jax.experimental import pallas as pl
from jax.experimental.pallas import tpu as pltpu
from jax.sharding import PartitionSpec as P

MESH = pl.DeviceIdType.MESH
VMEM = pltpu.VMEM
SMEM = pltpu.SMEM

SLOTS = 384
ROW_BLOCKS = 32
COL_BLOCKS = 64
FWD_PAIRS = 208
BWD_PAIRS = 224
UNROLL = 16
SPLIT_ROWS = 208
SEMS = 128
bf16, f32, i32 = jnp.bfloat16, jnp.float32, jnp.int32


def order_slots(key_lane, key_sub, other_sub, count, keys, empty):
    lane = lax.broadcasted_iota(i32, (1, SLOTS), 1)
    sub = lax.broadcasted_iota(i32, (SLOTS, 1), 0)
    key_l = jnp.where(lane < count, key_lane, -1)
    key_s = jnp.where(sub < count, key_sub, -2)
    before = (key_s == key_l) & (lane < sub)
    rank = jnp.sum(jnp.where(before, 1.0, 0.0), axis=1, keepdims=True)
    k_lane = lax.broadcasted_iota(i32, (1, 128), 1)
    k_sub = lax.broadcasted_iota(i32, (keys, 1), 0)
    in_lane = jnp.sum(jnp.where(key_s == k_lane, 1.0, 0.0), axis=0, keepdims=True)
    in_sub = jnp.sum(jnp.where(key_l == k_sub, 1.0, 0.0), axis=1, keepdims=True)
    pairs_l = jnp.floor((in_lane + 1.0) * 0.5)
    pairs_s = jnp.floor((in_sub + 1.0) * 0.5)
    begin = jnp.sum(jnp.where(k_lane < key_s, pairs_l, 0.0), axis=1, keepdims=True)
    place = jnp.where(sub < count, 2.0 * begin + rank, -1.0)
    begin_s = jnp.sum(jnp.where(k_lane < k_sub, pairs_l, 0.0), axis=1, keepdims=True)
    begin_l = jnp.sum(jnp.where(k_sub < k_lane, pairs_s, 0.0), axis=0, keepdims=True)
    spot = lax.broadcasted_iota(i32, (1, 512), 1).astype(f32)
    here = place == spot
    slot = SLOTS - jnp.sum(jnp.where(here, (SLOTS - sub).astype(f32), 0.0), axis=0, keepdims=True)
    other = jnp.sum(jnp.where(here, other_sub.astype(f32), 0.0), axis=0, keepdims=True)
    first = (begin_s == spot) & (pairs_s > 0.0)
    keep = 1.0 - jnp.sum(jnp.where(first, 1.0, 0.0), axis=0, keepdims=True)
    last = jnp.where(pairs_l > 0.0, begin_l + pairs_l - 1.0, float(empty))
    last = jnp.concatenate([last] * 4, axis=1)
    return jnp.concatenate([slot, other, keep, last], axis=0).astype(i32)


def plan_kernel(count_ref, row_l, col_l, row_s, col_s, out_ref):
    count = count_ref[0, 0]
    out_ref[0:4, :] = order_slots(row_l[...], row_s[...], col_s[...], count, ROW_BLOCKS, FWD_PAIRS)
    out_ref[4:8, :] = order_slots(col_l[...], col_s[...], row_s[...], count, COL_BLOCKS, BWD_PAIRS)


def plan(block_row, block_col, block_count):
    return pl.pallas_call(
        plan_kernel,
        out_shape=jax.ShapeDtypeStruct((8, 512), i32),
        in_specs=[pl.BlockSpec(memory_space=SMEM)] + [pl.BlockSpec(memory_space=VMEM)] * 4,
        out_specs=pl.BlockSpec(memory_space=VMEM),
        name="plan",
    )(
        block_count.reshape(1, 1),
        block_row.reshape(1, SLOTS),
        block_col.reshape(1, SLOTS),
        block_row.reshape(SLOTS, 1),
        block_col.reshape(SLOTS, 1),
    )


class Net:
    def __init__(self, send, recv):
        self.send, self.recv, self.started = send, recv, []

    def put(self, src, dst, device):
        at = len(self.started)
        copy = pltpu.make_async_remote_copy(
            src_ref=src,
            dst_ref=dst,
            send_sem=self.send.at[at],
            recv_sem=self.recv.at[at],
            device_id=device,
            device_id_type=MESH,
        )
        copy.start()
        self.started.append(copy)
        return copy

    def finish(self):
        for copy in self.started:
            copy.wait_send()


def layer_kernel(
    meta,
    feats,
    tiles_hbm,
    w_self_hbm,
    w_neigh_hbm,
    bias_ref,
    cot_hbm,
    act_out,
    gfeat_out,
    gself_out,
    gneigh_out,
    gbias_out,
    tiles,
    xg,
    prods,
    acc,
    degp,
    degs,
    degr,
    rowsum,
    bg,
    csend,
    crecv,
    csum,
    fwd_bufs,
    bwd_bufs,
    total,
    own_part,
    w_self,
    w_neigh,
    cot,
    neigh,
    grad_pre,
    wg,
    w1,
    w2,
    w3,
    w4,
    bias0,
    bias_s,
    rs_,
    rx_,
    rz_,
    rp_,
    rh_,
    rb_,
    wfull,
    send_sem,
    recv_sem,
    local_sem,
):
    gr, gc = lax.axis_index("gr"), lax.axis_index("gc")
    a, z, core = gr // 8, (gr // 2) % 4, gr % 2
    x, h = gc // 2, gc % 2

    def device(a_=None, z_=None, core_=None, x_=None, h_=None):
        a_ = a if a_ is None else a_
        z_ = z if z_ is None else z_
        core_ = core if core_ is None else core_
        x_ = x if x_ is None else x_
        h_ = h if h_ is None else h_
        return (a_ * 8 + z_ * 2 + core_, x_ * 2 + h_)

    sib = device(core_=1 - core)
    z_peer = {d: device(z_=(z + d) % 4) for d in (1, 2, 3)}
    x_peer = {d: device(x_=(x + d) % 4) for d in (1, 2, 3)}
    a_peer = device(a_=1 - a)
    h_peer = device(h_=1 - h)
    diagonal = {d: device(x_=(x + d) % 4, h_=1 - h) for d in (1, 2, 3)}

    loads = [
        pltpu.make_async_copy(tiles_hbm, tiles.at[pl.ds(0, SLOTS)], local_sem.at[0]),
        pltpu.make_async_copy(feats, xg.at[pl.ds(4 * gr, 4)], local_sem.at[1]),
        pltpu.make_async_copy(w_self_hbm, w_self, local_sem.at[2]),
        pltpu.make_async_copy(w_neigh_hbm, w_neigh, local_sem.at[3]),
        pltpu.make_async_copy(cot_hbm, cot, local_sem.at[4]),
    ]
    for copy in loads:
        copy.start()

    barrier = pltpu.get_barrier_semaphore()
    peers = [sib, a_peer, h_peer]
    peers += list(z_peer.values()) + list(x_peer.values()) + list(diagonal.values())
    for peer in peers:
        pl.semaphore_signal(barrier, inc=1, device_id=peer, device_id_type=MESH)
    pl.semaphore_wait(barrier, len(peers))
    net = Net(send_sem, recv_sem)

    def gather(buf, base, ring, side, up, down, across, own, forward, steps):
        def piece(d, other, j):
            return buf.at[pl.ds(base((ring + d) % 4, (1 - side) if other else side) + 2 * j, 2)]

        def push(d, other, j, device_id):
            return net.put(piece(d, other, j), piece(d, other, j), device_id)

        first = {0: {}, 1: {}}
        targets = (up, down, across)
        for j, way in ((0, 0), (1, 1), (1, 2), (0, 2), (1, 0), (0, 1)):
            first[j][way] = net.put(own(j), piece(0, 0, j), targets[way])
        own_sib = forward(0, 0, None)

        first[0][0].wait_recv()
        up_1 = push(3, 0, 0, up)
        across_0 = push(3, 0, 0, across)
        sent = [forward(3, 0, 0)]
        first[1][1].wait_recv()
        down_1 = push(1, 0, 1, down)
        across_1 = push(1, 0, 1, across)
        sent.append(forward(1, 0, 1))
        first[1][2].wait_recv()
        up_2 = push(0, 1, 1, up)
        sent.append(forward(0, 1, 1))
        first[0][2].wait_recv()
        down_2 = push(0, 1, 0, down)
        sent.append(forward(0, 1, 0))
        first[1][0].wait_recv()
        sent.append(forward(3, 0, 1))
        first[0][1].wait_recv()
        sent.append(forward(1, 0, 0))
        steps[0]()
        across_0.wait_recv()
        up_3 = push(3, 1, 0, up)
        sent.append(forward(3, 1, 0))
        across_1.wait_recv()
        down_3 = push(1, 1, 1, down)
        sent.append(forward(1, 1, 1))
        up_1.wait_recv()
        sent.append(forward(2, 0, 0))
        down_1.wait_recv()
        sent.append(forward(2, 0, 1))
        steps[1]()
        up_2.wait_recv()
        sent.append(forward(3, 1, 1))
        down_2.wait_recv()
        sent.append(forward(1, 1, 0))
        up_3.wait_recv()
        sent.append(forward(2, 1, 0))
        down_3.wait_recv()
        sent.append(forward(2, 1, 1))
        for copy in [own_sib] + sent:
            if copy is not None:
                copy.wait_recv()

    def scatter(bufs, src, at, ring, side, ring_peer, across, ready, steps):
        ra_buf, rb_buf, r2a_src, r2a_buf, r2b_src, r2b_buf = bufs
        top, low = pl.ds(0, SPLIT_ROWS), pl.ds(SPLIT_ROWS, 512 - SPLIT_ROWS)
        near, far, far_b = {}, {}, {}
        for d in (2, 1, 3, 0):
            ready(d, 1)
            far_b[d] = net.put(src.at[at(d, 1), low], rb_buf.at[d], across)
            if d:
                far[d] = net.put(src.at[at(d, 1), top], ra_buf.at[2 * d - 2], ring_peer[d])
        for d in (2, 1, 3, 0):
            ready(d, 0)
            if d:
                near[d] = net.put(src.at[at(d, 0), top], ra_buf.at[2 * d - 1], ring_peer[d])
        steps[0]()
        second = {}
        for d in (2, 1, 3):
            far_b[d].wait_recv()
            part = src[at(d, 0), low].astype(f32) + rb_buf[d].astype(f32)
            r2b_src[d - 1] = part.astype(bf16)
            second[d] = net.put(r2b_src.at[d - 1], r2b_buf.at[d - 1], ring_peer[d])
        part = src[at(0, 1), top].astype(f32)
        for d in (1, 3, 2):
            far[d].wait_recv()
            part += ra_buf[2 * d - 2].astype(f32)
        r2a_src[...] = part.astype(bf16)
        second_a = net.put(r2a_src, r2a_buf, across)
        part = src[at(0, 0), top].astype(f32)
        for d in (1, 3, 2):
            near[d].wait_recv()
            part += ra_buf[2 * d - 1].astype(f32)
        steps[1]()
        second_a.wait_recv()
        total[top, :] = part + r2a_buf[...].astype(f32)
        far_b[0].wait_recv()
        part = src[at(0, 0), low].astype(f32) + rb_buf[0].astype(f32)
        for d in (1, 3, 2):
            second[d].wait_recv()
            part += r2b_buf[d - 1].astype(f32)
        total[low, :] = part

    def multiply(base, source, backward, pairs):
        acc[...] = jnp.zeros_like(acc)
        prods[pairs] = jnp.zeros((128, 256), bf16)

        def body(step, carry):
            for u in range(UNROLL):
                p = step * UNROLL + u
                left = [tiles[meta[base, 2 * p + i]] for i in (0, 1)]
                right = jnp.concatenate([source[meta[base + 1, 2 * p + i]] for i in (0, 1)], axis=0)
                if backward:
                    left = jnp.concatenate(left, axis=0)
                    form = (((0,), (0,)), ((), ()))
                else:
                    left = jnp.concatenate(left, axis=1)
                    form = (((1,), (0,)), ((), ()))
                product = lax.dot_general(left, right, form, preferred_element_type=f32)
                running = product + jnp.where(meta[base + 2, p] != 0, acc[...], 0.0)
                acc[...] = running
                prods[p] = running.astype(bf16)
            return carry

        lax.fori_loop(0, pairs // UNROLL, body, 0)

    def count_some(begin, end):
        ones = jnp.ones((8, 256), bf16)

        def body(step, carry):
            for u in range(UNROLL):
                p = step * UNROLL + u
                pair = jnp.concatenate([tiles[meta[0, 2 * p + i]] for i in (0, 1)], axis=1)
                present = jnp.where(pair != 0, jnp.ones((), bf16), jnp.zeros((), bf16))
                found = lax.dot_general(
                    ones, present, (((1,), (1,)), ((), ())), preferred_element_type=f32
                )
                running = found + jnp.where(meta[2, p] != 0, degp[FWD_PAIRS], 0.0)
                degp[FWD_PAIRS] = running
                degp[p] = running
            return carry

        lax.fori_loop(begin, end, body, 0)

    def count_first():
        loads[0].wait()
        tiles[SLOTS] = jnp.zeros((128, 128), bf16)
        degp[FWD_PAIRS] = jnp.zeros((8, 128), f32)
        count_some(0, 7)

    degree_copies = []

    def count_last():
        count_some(7, 13)
        degp[FWD_PAIRS] = jnp.zeros((8, 128), f32)
        sub = lax.broadcasted_iota(i32, (8, 128), 0)
        for g in range(8):
            rows = jnp.zeros((8, 128), f32)
            for j in range(4):
                rows = jnp.where(sub == j, degp[meta[3, 4 * g + j]], rows)
            degs[g] = rows
        for d in range(4):
            for e in (0, 1):
                if (d, e) == (0, 0):
                    continue
                target = h_peer if d == 0 else (diagonal[d] if e else x_peer[d])
                index = ((x + d) % 4) * 2 + ((1 - h) if e else h)
                degree_copies.append(net.put(degs.at[index], degr.at[2 * d + e], target))
        for copy in loads[1:]:
            copy.wait()
        for j in range(4):
            own_part[pl.ds(128 * j, 128), :] = (
                jnp.dot(xg[4 * gr + j], w_self[...], preferred_element_type=f32) + bias_ref[...]
            )

    def to_sibling(d, other, j):
        if j is None:
            own = xg.at[pl.ds(4 * gr, 4)]
            return net.put(feats, own, sib)
        at = 4 * ((1 - a if other else a) * 8 + ((z + d) % 4) * 2 + core) + 2 * j
        return net.put(xg.at[pl.ds(at, 2)], xg.at[pl.ds(at, 2)], sib)

    gather(
        xg,
        lambda ring, side: 4 * (side * 8 + ring * 2 + core),
        z,
        a,
        z_peer[1],
        z_peer[3],
        a_peer,
        lambda j: feats.at[pl.ds(2 * j, 2)],
        to_sibling,
        (count_first, count_last),
    )

    multiply(0, xg, False, FWD_PAIRS)

    def rows_at(d, other):
        return ((x + d) % 4) * 2 + ((1 - h) if other else h)

    def rows_ready(d, other):
        shard = rows_at(d, other)
        for j in range(4):
            rowsum[shard, pl.ds(128 * j, 128), :] = prods[meta[3, 4 * shard + j]]

    def nothing():
        pass

    scatter(fwd_bufs, rowsum, rows_at, x, h, x_peer, h_peer, rows_ready, (nothing, nothing))

    degree = degs[gc]
    for copy in degree_copies:
        copy.wait_recv()
    for slot in range(1, 8):
        degree += degr[slot]
    degree = jnp.maximum(degree, 1.0)
    gathered = {}
    for j in range(4):
        rows = pl.ds(128 * j, 128)
        counts = jnp.broadcast_to(degree[j : j + 1, :], (128, 128)).T
        counts = jnp.concatenate([counts, counts], axis=1)
        mean = (total[rows, :] / counts).astype(bf16)
        neigh[rows, :] = mean
        preact = own_part[rows, :] + jnp.dot(mean, w_neigh[...], preferred_element_type=f32)
        sigma = jax.nn.sigmoid(preact)
        act_out[rows, :] = (preact * sigma).astype(bf16)
        grad = cot[rows, :].astype(f32) * sigma * (1.0 + preact * (1.0 - sigma))
        grad = grad.astype(bf16)
        grad_pre[rows, :] = grad
        projected = lax.dot_general(
            grad, w_neigh[...], (((1,), (1,)), ((), ())), preferred_element_type=f32
        )
        bg[4 * gc + j] = (projected / counts).astype(bf16)

    contract_rows = (((0,), (0,)), ((), ()))
    state = {}

    def weight_grads():
        own = jnp.concatenate([xg[4 * gr + j] for j in range(4)], axis=0)
        grad = grad_pre[...]
        wg[0:256, :] = lax.dot_general(own, grad, contract_rows, preferred_element_type=f32)
        wg[256:512, :] = lax.dot_general(
            neigh[...], grad, contract_rows, preferred_element_type=f32
        )
        bias0[...] = jnp.broadcast_to(
            jnp.sum(grad.astype(f32), axis=0, keepdims=True), (8, 256)
        )
        state["s"] = [
            net.put(wg.at[pl.ds((1 - core) * 256, 256)], rs_, sib),
            net.put(bias0, rb_.at[0], sib),
        ]
        own_part[...] = lax.dot_general(
            grad, w_self[...], (((1,), (1,)), ((), ())), preferred_element_type=f32
        )

    def sum_sib():
        for copy in state["s"]:
            copy.wait_recv()
        w1[...] = wg[pl.ds(core * 256, 256), :] + rs_[...]
        bias_s[0] = bias0[...] + rb_[0]
        state["x"] = []
        for d in (2, 1, 3):
            src = w1.at[pl.ds(((x + d) % 4) * 64, 64)]
            state["x"].append(net.put(src, rx_.at[d - 1], x_peer[d]))
            state["x"].append(net.put(bias_s.at[0], rb_.at[d], x_peer[d]))

    def sum_x():
        for copy in state["x"]:
            copy.wait_recv()
        w2[...] = w1[pl.ds(x * 64, 64), :] + rx_[0] + rx_[1] + rx_[2]
        bias_s[1] = bias_s[0] + rb_[1] + rb_[2] + rb_[3]
        state["z"] = []
        for d in (2, 1, 3):
            src = w2.at[pl.ds(((z + d) % 4) * 16, 16)]
            state["z"].append(net.put(src, rz_.at[d - 1], z_peer[d]))
            state["z"].append(net.put(bias_s.at[1], rb_.at[3 + d], z_peer[d]))

    def sum_z():
        for copy in state["z"]:
            copy.wait_recv()
        w3[...] = w2[pl.ds(z * 16, 16), :] + rz_[0] + rz_[1] + rz_[2]
        bias_s[2] = bias_s[1] + rb_[4] + rb_[5] + rb_[6]
        state["p"] = [
            net.put(w3.at[pl.ds((1 - a) * 8, 8)], rp_, a_peer),
            net.put(bias_s.at[2], rb_.at[7], a_peer),
        ]

    def sum_p():
        for copy in state["p"]:
            copy.wait_recv()
        w4[...] = w3[pl.ds(a * 8, 8), :] + rp_[...]
        bias_s[3] = bias_s[2] + rb_[7]
        state["h"] = [net.put(w4, rh_, h_peer), net.put(bias_s.at[3], rb_.at[8], h_peer)]

    def share(rows, size, targets):
        part = wfull.at[pl.ds(rows, size)]
        return [net.put(part, part, target) for target in targets]

    def sum_h():
        for copy in state["h"]:
            copy.wait_recv()
        wfull[pl.ds(core * 256 + x * 64 + z * 16 + a * 8, 8), :] = w4[...] + rh_[...]
        gbias_out[...] = (bias_s[3] + rb_[8])[0:1, :] * (1.0 / 256.0)
        state["gp"] = share(core * 256 + x * 64 + z * 16 + a * 8, 8, [a_peer])

    def share_z():
        for copy in state["gp"]:
            copy.wait_recv()
        state["gz"] = share(core * 256 + x * 64 + z * 16, 16, list(z_peer.values()))

    def share_x():
        for copy in state["gz"]:
            copy.wait_recv()
        state["gx"] = share(core * 256 + x * 64, 64, list(x_peer.values()))

    def share_sib():
        for copy in state["gx"]:
            copy.wait_recv()
        state["gs"] = share(core * 256, 256, [sib])

    def mid_gather():
        sum_sib()

    def late_gather():
        sum_x()

    def no_forward(d, other, j):
        if j is None:
            weight_grads()
        return None

    gather(
        bg,
        lambda ring, side: 4 * (ring * 2 + side),
        x,
        h,
        x_peer[1],
        x_peer[3],
        h_peer,
        lambda j: bg.at[pl.ds(4 * gc + 2 * j, 2)],
        no_forward,
        (mid_gather, late_gather),
    )
    sum_z()

    multiply(4, bg, True, BWD_PAIRS)
    sum_p()

    def cols_at(d, other):
        return ((z + d) % 4) * 2 + ((1 - a) if other else a)

    def block_of(d, other, core_):
        return 4 * (((1 - a) if other else a) * 8 + ((z + d) % 4) * 2 + core_)

    to_sib = {}
    for other in (1, 0):
        for d in (2, 1, 3, 0):
            shard = cols_at(d, other)
            for j in range(4):
                csend[shard, pl.ds(128 * j, 128), :] = prods[
                    meta[7, block_of(d, other, 1 - core) + j]
                ]
            to_sib[d, other] = net.put(csend.at[shard], crecv.at[shard], sib)

    def cols_ready(d, other):
        shard = cols_at(d, other)
        to_sib[d, other].wait_recv()
        for j in range(4):
            rows = pl.ds(128 * j, 128)
            mine = prods[meta[7, block_of(d, other, core) + j]].astype(f32)
            csum[shard, rows, :] = (mine + crecv[shard, rows, :].astype(f32)).astype(bf16)

    def mid_scatter():
        sum_h()

    def late_scatter():
        share_z()

    scatter(bwd_bufs, csum, cols_at, z, a, z_peer, a_peer, cols_ready, (mid_scatter, late_scatter))
    share_x()
    gfeat_out[...] = (own_part[...] + total[...]).astype(bf16)
    share_sib()
    for copy in state["gs"]:
        copy.wait_recv()
    gself_out[...] = wfull[0:256, :] * (1.0 / 256.0)
    gneigh_out[...] = wfull[256:512, :] * (1.0 / 256.0)
    net.finish()


def layer(meta, features, tiles, w_self, w_neigh, bias, cotangent):
    low = 512 - SPLIT_ROWS
    scatter_bufs = [
        VMEM((6, SPLIT_ROWS, 256), bf16),
        VMEM((4, low, 256), bf16),
        VMEM((SPLIT_ROWS, 256), bf16),
        VMEM((SPLIT_ROWS, 256), bf16),
        VMEM((3, low, 256), bf16),
        VMEM((3, low, 256), bf16),
    ]
    scratch = [
        VMEM((SLOTS + 1, 128, 128), bf16),
        VMEM((COL_BLOCKS, 128, 256), bf16),
        VMEM((BWD_PAIRS + 1, 128, 256), bf16),
        VMEM((128, 256), f32),
        VMEM((FWD_PAIRS + 1, 8, 128), f32),
        VMEM((8, 8, 128), f32),
        VMEM((8, 8, 128), f32),
        VMEM((8, 512, 256), bf16),
        VMEM((ROW_BLOCKS, 128, 256), bf16),
        VMEM((8, 512, 256), bf16),
        VMEM((8, 512, 256), bf16),
        VMEM((8, 512, 256), bf16),
        scatter_bufs,
        scatter_bufs,
        VMEM((512, 256), f32),
        VMEM((512, 256), f32),
        VMEM((256, 256), bf16),
        VMEM((256, 256), bf16),
        VMEM((512, 256), bf16),
        VMEM((512, 256), bf16),
        VMEM((512, 256), bf16),
        VMEM((512, 256), f32),
        VMEM((256, 256), f32),
        VMEM((64, 256), f32),
        VMEM((16, 256), f32),
        VMEM((8, 256), f32),
        VMEM((8, 256), f32),
        VMEM((4, 8, 256), f32),
        VMEM((256, 256), f32),
        VMEM((3, 64, 256), f32),
        VMEM((3, 16, 256), f32),
        VMEM((8, 256), f32),
        VMEM((8, 256), f32),
        VMEM((9, 8, 256), f32),
        VMEM((512, 256), f32),
        pltpu.SemaphoreType.DMA((SEMS,)),
        pltpu.SemaphoreType.DMA((SEMS,)),
        pltpu.SemaphoreType.DMA((5,)),
    ]
    anywhere = pl.BlockSpec(memory_space=pl.ANY)
    return pl.pallas_call(
        layer_kernel,
        out_shape=(
            jax.ShapeDtypeStruct((512, 256), bf16),
            jax.ShapeDtypeStruct((512, 256), bf16),
            jax.ShapeDtypeStruct((256, 256), f32),
            jax.ShapeDtypeStruct((256, 256), f32),
            jax.ShapeDtypeStruct((1, 256), f32),
        ),
        in_specs=[
            pl.BlockSpec(memory_space=SMEM),
            anywhere,
            anywhere,
            anywhere,
            anywhere,
            pl.BlockSpec(memory_space=VMEM),
            anywhere,
        ],
        out_specs=[pl.BlockSpec(memory_space=VMEM)] * 5,
        scratch_shapes=scratch,
        compiler_params=pltpu.CompilerParams(
            collective_id=0, has_side_effects=True, vmem_limit_bytes=60 * 1024 * 1024
        ),
        name="layer",
    )(meta, features, tiles, w_self, w_neigh, bias, cotangent)


def local(
    features,
    block_values,
    block_row,
    block_col,
    block_count,
    weight_self,
    weight_neigh,
    bias,
    cotangent,
):
    meta = plan(block_row, block_col, block_count)
    activations, grad_features, grad_self, grad_neigh, grad_bias = layer(
        meta,
        features.reshape(4, 128, 256),
        block_values.reshape(SLOTS, 128, 128),
        weight_self,
        weight_neigh,
        bias.reshape(1, 256),
        cotangent,
    )
    return (activations, grad_features, grad_self, grad_neigh, grad_bias.reshape(256))


def solution(mesh):
    placed = (
        P(("gr", "gc"), None),
        P("gr", "gc", None, None, None),
        P("gr", "gc", None),
        P("gr", "gc", None),
        P("gr", "gc"),
        P(),
        P(),
        P(),
        P(("gr", "gc"), None),
    )
    return jax.shard_map(
        local,
        mesh=mesh,
        in_specs=placed,
        out_specs=(P(("gr", "gc"), None), P(("gr", "gc"), None), P(), P(), P()),
        check_vma=False,
    )
```

time: 634 us -> 126 us (0.20); the launches traced: 625 us -> 124 us
  matrix products: 301 us -> 0 us
  waiting for transfers between devices: 125 us -> 0 us
  Pallas kernels: 0 us -> 112 us
  blocking collectives: 112 us -> 0 us
  local copies, waits for them, and re-layouts: 42.9 us -> 10.9 us
  loops' own time: 15.1 us -> 0 us
  between operations: 15.6 us -> 1.29 us
  other arithmetic: 12.4 us -> 0 us
    dot_general x43 -> x0, matrix products: 301 us -> none  [the longest x12 165 us: step(): jnp.einsum('gb,gif->bif', put_onehot, prods, precision=lax.Precision.HIGH...]
    pallas_call x0 -> x2, Pallas kernels: none -> 112 us  [the longest x1 109 us: layer(): pl.pallas_call(layer_kernel, out_shape=(jax.ShapeDtypeStruct((512, 256),...]
    all_gather x2 -> x0, waiting for transfers between devices: 91.4 us -> none  [the longest x1 51.8 us: local(): row_back = lax.all_gather(back_rows, 'gc', axis=0, tiled=True)]
    psum x1 -> x0, blocking collectives: 70.4 us -> none  [local(): lax.psum((local_self, local_neigh, local_bias), ('gr', 'gc'))]
    unnamed x1 -> x0, blocking collectives: 42 us -> none
    while x38 -> x0, local copies, waits for them, and re-layouts: 37.4 us -> none
    reduce_scatter x2 -> x0, waiting for transfers between devices: 33.2 us -> none  [the longest x1 32.1 us: local(): lax.psum_scatter(partial_rows, 'gc', scatter_dimension=0, tiled=True)]
    another operation x2 -> x0, loops' own time: 15.1 us -> none  [block_pass(): total = lax.fori_loop(0, slots // group, step, total)]
  transfers between devices with their start and end apart: 5 -> 0, of which waited for: 4 -> 0; matrix products, arithmetic and copies ran while one was open for 25% -> 0% of each run, Pallas kernels for 0% -> 0%
where the time goes in v1:
time: 126 us; the launch traced here: 124 us
  Pallas kernels  112 us (89%)
  local copies, waits for them, and re-layouts  10.9 us (9%)
  between operations  1.29 us (1%)
    pallas_call x1, Pallas kernels, layer(): pl.pallas_call(layer_kernel, out_shape=(jax.ShapeDtypeStruct((512, 256),...  109 us
    unnamed x5, local copies, waits for them, and re-layouts  7.92 us

profile of v1, /device:TPU:0, one launch (start us, length us, event | category | flops | bytes accessed | tf_op | source)
XLA Modules:
  0.0 124.0 jit_solution(9190307003571053615)
XLA Ops:
  1.3 1.5 %copy.15.col_s = s32[384,1]{1,0:T(8,128)} copy(s32[384,1]{0,1:T(1,128)} %bitcast.12) | data formatting | bytes 3072 | tf_op jit(solution)/shard_map/reshape | solution.py:71
  2.8 1.5 %copy.14.row_s = s32[384,1]{1,0:T(8,128)} copy(s32[384,1]{0,1:T(1,128)} %bitcast.10) | data formatting | bytes 3072 | tf_op jit(solution)/shard_map/reshape | solution.py:70
  4.3 2.4 %plan.1.meta = s32[8,512]{1,0:T(8,128)} custom-call(s32[1,1]{1,0:T(1,128)S(6)} %copy.21.count_ref, s32[1,384]{1,0:T(1,128)} %bitcast.11, s32[1,384]{1,0:T(1,128)} %bitcast.13, s32[384,1]{1,0:T(8,128)} %copy.14.row_s, s32[384,1]{1,0:T(8,128)} %copy.15.col_s), custom_call_target="tpu_custom_call" | custom-call | tf_op jit(solution)/shard_map/plan/pallas_call | solution.py:60
  6.7 109.4 %layer.1 = (bf16[512,256]{1,0:T(8,128)(2,1)}, bf16[512,256]{1,0:T(8,128)(2,1)}, f32[256,256]{1,0:T(8,128)}, f32[256,256]{1,0:T(8,128)}, f32[1,256]{1,0:T(1,128)}) custom-call(s32[8,512]{1,0:T(8,128)} %plan.1.meta, bf16[4,128,256]{2,1,0:T(8,128)(2,1)} %bitcast.9, bf16[384,128,128]{2,1,0:T(8,128)(2,1)} %bitcast.8, bf16[256,256]{1,0:T(8,128)(2,1)} %w_self_hbm.1, ...), custom_call_target="tpu_custom_call" | custom-call | tf_op jit(solution)/shard_map/layer/pallas_call | solution.py:619
  116.1 1.7 %copy.22 = bf16[512,256]{1,0:T(8,128)(2,1)} copy(bf16[512,256]{1,0:T(8,128)(2,1)} %get-tuple-element.20) | data formatting | bytes 524288
  117.7 1.7 %copy.23 = bf16[512,256]{1,0:T(8,128)(2,1)} copy(bf16[512,256]{1,0:T(8,128)(2,1)} %get-tuple-element.21) | data formatting | bytes 524288
  119.4 1.7 %copy.24 = f32[256,256]{1,0:T(8,128)} copy(f32[256,256]{1,0:T(8,128)} %get-tuple-element.22) | data formatting | bytes 524288
  121.1 1.7 %copy.25 = f32[256,256]{1,0:T(8,128)} copy(f32[256,256]{1,0:T(8,128)} %get-tuple-element.23) | data formatting | bytes 524288
  122.8 1.2 %copy.26 = f32[256]{0:T(256)} copy(f32[256]{0:T(256)} %bitcast.14) | data formatting | bytes 2048

commit v2 on v1

--- a/solution.py
+++ b/solution.py
@@ -16,60 +16,47 @@
 COL_BLOCKS = 64
 FWD_PAIRS = 208
 BWD_PAIRS = 224
-UNROLL = 16
+FWD_UNROLL = 26
+BWD_UNROLL = 28
 SPLIT_ROWS = 208
-SEMS = 128
+SEMS = 192
 bf16, f32, i32 = jnp.bfloat16, jnp.float32, jnp.int32
 
 
-def order_slots(key_lane, key_sub, other_sub, count, keys, empty):
+def count_where(mask, axis, values=1):
+    return jnp.sum(jnp.where(mask, values, 0), axis=axis, keepdims=True, dtype=i32)
+
+
+def order_slots(key_lane, key_sub, other_sub, count, keys, others, empty):
     lane = lax.broadcasted_iota(i32, (1, SLOTS), 1)
     sub = lax.broadcasted_iota(i32, (SLOTS, 1), 0)
     key_l = jnp.where(lane < count, key_lane, -1)
     key_s = jnp.where(sub < count, key_sub, -2)
-    before = (key_s == key_l) & (lane < sub)
-    rank = jnp.sum(jnp.where(before, 1.0, 0.0), axis=1, keepdims=True)
+    rank = count_where((key_s == key_l) & (lane < sub), 1)
     k_lane = lax.broadcasted_iota(i32, (1, 128), 1)
     k_sub = lax.broadcasted_iota(i32, (keys, 1), 0)
-    in_lane = jnp.sum(jnp.where(key_s == k_lane, 1.0, 0.0), axis=0, keepdims=True)
-    in_sub = jnp.sum(jnp.where(key_l == k_sub, 1.0, 0.0), axis=1, keepdims=True)
-    pairs_l = jnp.floor((in_lane + 1.0) * 0.5)
-    pairs_s = jnp.floor((in_sub + 1.0) * 0.5)
-    begin = jnp.sum(jnp.where(k_lane < key_s, pairs_l, 0.0), axis=1, keepdims=True)
-    place = jnp.where(sub < count, 2.0 * begin + rank, -1.0)
-    begin_s = jnp.sum(jnp.where(k_lane < k_sub, pairs_l, 0.0), axis=1, keepdims=True)
-    begin_l = jnp.sum(jnp.where(k_sub < k_lane, pairs_s, 0.0), axis=0, keepdims=True)
-    spot = lax.broadcasted_iota(i32, (1, 512), 1).astype(f32)
+    pairs_l = (count_where(key_s == k_lane, 0) + 1) >> 1
+    pairs_s = (count_where(key_l == k_sub, 1) + 1) >> 1
+    begin = count_where(k_lane < key_s, 1, pairs_l)
+    place = jnp.where(sub < count, 2 * begin + rank, -1)
+    begin_s = count_where(k_lane < k_sub, 1, pairs_l)
+    begin_l = count_where(k_sub < k_lane, 0, pairs_s)
+    spot = lax.broadcasted_iota(i32, (1, 512), 1)
     here = place == spot
-    slot = SLOTS - jnp.sum(jnp.where(here, (SLOTS - sub).astype(f32), 0.0), axis=0, keepdims=True)
-    other = jnp.sum(jnp.where(here, other_sub.astype(f32), 0.0), axis=0, keepdims=True)
-    first = (begin_s == spot) & (pairs_s > 0.0)
-    keep = 1.0 - jnp.sum(jnp.where(first, 1.0, 0.0), axis=0, keepdims=True)
-    last = jnp.where(pairs_l > 0.0, begin_l + pairs_l - 1.0, float(empty))
+    slot = SLOTS - count_where(here, 0, SLOTS - sub)
+    other = count_where(here, 0, other_sub)
+    first = (begin_s == spot) & (pairs_s > 0)
+    keep = 1 - count_where(first, 0)
+    last = jnp.where(pairs_l > 0, begin_l + pairs_l - 1, empty)
     last = jnp.concatenate([last] * 4, axis=1)
-    return jnp.concatenate([slot, other, keep, last], axis=0).astype(i32)
-
-
-def plan_kernel(count_ref, row_l, col_l, row_s, col_s, out_ref):
-    count = count_ref[0, 0]
-    out_ref[0:4, :] = order_slots(row_l[...], row_s[...], col_s[...], count, ROW_BLOCKS, FWD_PAIRS)
-    out_ref[4:8, :] = order_slots(col_l[...], col_s[...], row_s[...], count, COL_BLOCKS, BWD_PAIRS)
-
-
-def plan(block_row, block_col, block_count):
-    return pl.pallas_call(
-        plan_kernel,
-        out_shape=jax.ShapeDtypeStruct((8, 512), i32),
-        in_specs=[pl.BlockSpec(memory_space=SMEM)] + [pl.BlockSpec(memory_space=VMEM)] * 4,
-        out_specs=pl.BlockSpec(memory_space=VMEM),
-        name="plan",
-    )(
-        block_count.reshape(1, 1),
-        block_row.reshape(1, SLOTS),
-        block_col.reshape(1, SLOTS),
-        block_row.reshape(SLOTS, 1),
-        block_col.reshape(SLOTS, 1),
-    )
+    slot = jnp.clip(slot, 0, SLOTS)
+    other = jnp.clip(other, 0, others - 1)
+    last = jnp.clip(last, 0, empty)
+    return jnp.concatenate([slot, other, keep, last], axis=0)
+
+
+def as_column(row):
+    return jnp.broadcast_to(row, (128, SLOTS)).T[:, 0:1]
 
 
 class Net:
@@ -91,12 +78,15 @@
         return copy
 
     def finish(self):
+        assert len(self.started) <= SEMS
         for copy in self.started:
             copy.wait_send()
 
 
 def layer_kernel(
-    meta,
+    count_ref,
+    row_ref,
+    col_ref,
     feats,
     tiles_hbm,
     w_self_hbm,
@@ -105,9 +95,12 @@
     cot_hbm,
     act_out,
     gfeat_out,
-    gself_out,
-    gneigh_out,
+    gweight_out,
     gbias_out,
+    meta_v,
+    meta,
+    act_v,
+    gfeat_v,
     tiles,
     xg,
     prods,
@@ -184,58 +177,44 @@
     pl.semaphore_wait(barrier, len(peers))
     net = Net(send_sem, recv_sem)
 
-    def gather(buf, base, ring, side, up, down, across, own, forward, steps):
-        def piece(d, other, j):
-            return buf.at[pl.ds(base((ring + d) % 4, (1 - side) if other else side) + 2 * j, 2)]
+    def gather(buf, base, ring, side, ring_peer, across, own, forward, steps):
+        def piece(d, other, j, size=1):
+            return buf.at[pl.ds(base((ring + d) % 4, (1 - side) if other else side) + j, size)]
 
         def push(d, other, j, device_id):
             return net.put(piece(d, other, j), piece(d, other, j), device_id)
 
-        first = {0: {}, 1: {}}
-        targets = (up, down, across)
-        for j, way in ((0, 0), (1, 1), (1, 2), (0, 2), (1, 0), (0, 1)):
-            first[j][way] = net.put(own(j), piece(0, 0, j), targets[way])
-        own_sib = forward(0, 0, None)
-
-        first[0][0].wait_recv()
-        up_1 = push(3, 0, 0, up)
-        across_0 = push(3, 0, 0, across)
-        sent = [forward(3, 0, 0)]
-        first[1][1].wait_recv()
-        down_1 = push(1, 0, 1, down)
-        across_1 = push(1, 0, 1, across)
-        sent.append(forward(1, 0, 1))
-        first[1][2].wait_recv()
-        up_2 = push(0, 1, 1, up)
-        sent.append(forward(0, 1, 1))
-        first[0][2].wait_recv()
-        down_2 = push(0, 1, 0, down)
-        sent.append(forward(0, 1, 0))
-        first[1][0].wait_recv()
-        sent.append(forward(3, 0, 1))
-        first[0][1].wait_recv()
-        sent.append(forward(1, 0, 0))
+        come = {}
+        for j in range(4):
+            for d in (2, 0, 1, 3):
+                target = ring_peer[d] if d else across
+                come[(4 - d) % 4, 0 if d else 1, j] = net.put(own(j), piece(0, 0, j), target)
         steps[0]()
-        across_0.wait_recv()
-        up_3 = push(3, 1, 0, up)
-        sent.append(forward(3, 1, 0))
-        across_1.wait_recv()
-        down_3 = push(1, 1, 1, down)
-        sent.append(forward(1, 1, 1))
-        up_1.wait_recv()
-        sent.append(forward(2, 0, 0))
-        down_1.wait_recv()
-        sent.append(forward(2, 0, 1))
+        come[3, 0, 0].wait_recv()
+        come[3, 1, 0] = push(3, 0, 0, across)
+        come[1, 0, 0].wait_recv()
+        come[1, 1, 0] = push(1, 0, 0, across)
         steps[1]()
-        up_2.wait_recv()
-        sent.append(forward(3, 1, 1))
-        down_2.wait_recv()
-        sent.append(forward(1, 1, 0))
-        up_3.wait_recv()
-        sent.append(forward(2, 1, 0))
-        down_3.wait_recv()
-        sent.append(forward(2, 1, 1))
-        for copy in [own_sib] + sent:
+        for j in range(4):
+            come[2, 0, j].wait_recv()
+            come[2, 1, j] = push(2, 0, j, across)
+            if j:
+                come[0, 1, j].wait_recv()
+                come[3, 1, j] = push(0, 1, j, ring_peer[1])
+                come[1, 1, j] = push(0, 1, j, ring_peer[3])
+        sent = [forward(0, 0), forward(2, 0)]
+        come[0, 1, 0].wait_recv()
+        sent.append(forward(0, 1))
+        for d in (1, 3):
+            for j in (1, 2, 3):
+                come[d, 0, j].wait_recv()
+            sent.append(forward(d, 0))
+        steps[2]()
+        for d in (1, 3, 2):
+            for j in range(4):
+                come[d, 1, j].wait_recv()
+            sent.append(forward(d, 1))
+        for copy in sent:
             if copy is not None:
                 copy.wait_recv()
 
@@ -269,23 +248,25 @@
         for d in (1, 3, 2):
             near[d].wait_recv()
             part += ra_buf[2 * d - 1].astype(f32)
+        total[top, :] = part
         steps[1]()
-        second_a.wait_recv()
-        total[top, :] = part + r2a_buf[...].astype(f32)
         far_b[0].wait_recv()
         part = src[at(0, 0), low].astype(f32) + rb_buf[0].astype(f32)
+        steps[2]()
+        second_a.wait_recv()
+        total[top, :] += r2a_buf[...].astype(f32)
         for d in (1, 3, 2):
             second[d].wait_recv()
             part += r2b_buf[d - 1].astype(f32)
         total[low, :] = part
 
-    def multiply(base, source, backward, pairs):
-        acc[...] = jnp.zeros_like(acc)
-        prods[pairs] = jnp.zeros((128, 256), bf16)
+    def multiply(base, source, backward, unroll, begin, end):
+        if begin == 0:
+            acc[...] = jnp.zeros_like(acc)
 
         def body(step, carry):
-            for u in range(UNROLL):
-                p = step * UNROLL + u
+            for u in range(unroll):
+                p = step * unroll + u
                 left = [tiles[meta[base, 2 * p + i]] for i in (0, 1)]
                 right = jnp.concatenate([source[meta[base + 1, 2 * p + i]] for i in (0, 1)], axis=0)
                 if backward:
@@ -300,14 +281,14 @@
                 prods[p] = running.astype(bf16)
             return carry
 
-        lax.fori_loop(0, pairs // UNROLL, body, 0)
+        lax.fori_loop(begin, end, body, 0)
 
     def count_some(begin, end):
         ones = jnp.ones((8, 256), bf16)
 
         def body(step, carry):
-            for u in range(UNROLL):
-                p = step * UNROLL + u
+            for u in range(FWD_UNROLL):
+                p = step * FWD_UNROLL + u
                 pair = jnp.concatenate([tiles[meta[0, 2 * p + i]] for i in (0, 1)], axis=1)
                 present = jnp.where(pair != 0, jnp.ones((), bf16), jnp.zeros((), bf16))
                 found = lax.dot_general(
@@ -320,16 +301,28 @@
 
         lax.fori_loop(begin, end, body, 0)
 
+    def make_plan():
+        count = count_ref[0, 0]
+        row_l, col_l = row_ref[...], col_ref[...]
+        row_s, col_s = as_column(row_l), as_column(col_l)
+        meta_v[0:4, :] = order_slots(row_l, row_s, col_s, count, ROW_BLOCKS, COL_BLOCKS, FWD_PAIRS)
+        meta_v[4:8, :] = order_slots(col_l, col_s, row_s, count, COL_BLOCKS, ROW_BLOCKS, BWD_PAIRS)
+        copy = pltpu.make_async_copy(meta_v, meta, local_sem.at[5])
+        copy.start()
+        tiles[SLOTS] = jnp.zeros((128, 128), bf16)
+        prods[FWD_PAIRS] = jnp.zeros((128, 256), bf16)
+        degp[FWD_PAIRS] = jnp.zeros((8, 128), f32)
+        copy.wait()
+
     def count_first():
         loads[0].wait()
-        tiles[SLOTS] = jnp.zeros((128, 128), bf16)
-        degp[FWD_PAIRS] = jnp.zeros((8, 128), f32)
-        count_some(0, 7)
+        loads[1].wait()
+        count_some(0, 4)
 
     degree_copies = []
 
     def count_last():
-        count_some(7, 13)
+        count_some(4, 8)
         degp[FWD_PAIRS] = jnp.zeros((8, 128), f32)
         sub = lax.broadcasted_iota(i32, (8, 128), 0)
         for g in range(8):
@@ -344,34 +337,30 @@
                 target = h_peer if d == 0 else (diagonal[d] if e else x_peer[d])
                 index = ((x + d) % 4) * 2 + ((1 - h) if e else h)
                 degree_copies.append(net.put(degs.at[index], degr.at[2 * d + e], target))
-        for copy in loads[1:]:
+        for copy in loads[2:]:
             copy.wait()
         for j in range(4):
             own_part[pl.ds(128 * j, 128), :] = (
                 jnp.dot(xg[4 * gr + j], w_self[...], preferred_element_type=f32) + bias_ref[...]
             )
 
-    def to_sibling(d, other, j):
-        if j is None:
-            own = xg.at[pl.ds(4 * gr, 4)]
-            return net.put(feats, own, sib)
-        at = 4 * ((1 - a if other else a) * 8 + ((z + d) % 4) * 2 + core) + 2 * j
-        return net.put(xg.at[pl.ds(at, 2)], xg.at[pl.ds(at, 2)], sib)
+    def to_sibling(d, other):
+        at = 4 * ((1 - a if other else a) * 8 + ((z + d) % 4) * 2 + core)
+        return net.put(xg.at[pl.ds(at, 4)], xg.at[pl.ds(at, 4)], sib)
 
     gather(
         xg,
         lambda ring, side: 4 * (side * 8 + ring * 2 + core),
         z,
         a,
-        z_peer[1],
-        z_peer[3],
+        z_peer,
         a_peer,
-        lambda j: feats.at[pl.ds(2 * j, 2)],
+        lambda j: feats.at[pl.ds(j, 1)],
         to_sibling,
-        (count_first, count_last),
+        (make_plan, count_first, count_last),
     )
 
-    multiply(0, xg, False, FWD_PAIRS)
+    multiply(0, xg, False, FWD_UNROLL, 0, 8)
 
     def rows_at(d, other):
         return ((x + d) % 4) * 2 + ((1 - h) if other else h)
@@ -384,7 +373,7 @@
     def nothing():
         pass
 
-    scatter(fwd_bufs, rowsum, rows_at, x, h, x_peer, h_peer, rows_ready, (nothing, nothing))
+    scatter(fwd_bufs, rowsum, rows_at, x, h, x_peer, h_peer, rows_ready, (nothing,) * 3)
 
     degree = degs[gc]
     for copy in degree_copies:
@@ -401,7 +390,7 @@
         neigh[rows, :] = mean
         preact = own_part[rows, :] + jnp.dot(mean, w_neigh[...], preferred_element_type=f32)
         sigma = jax.nn.sigmoid(preact)
-        act_out[rows, :] = (preact * sigma).astype(bf16)
+        act_v[rows, :] = (preact * sigma).astype(bf16)
         grad = cot[rows, :].astype(f32) * sigma * (1.0 + preact * (1.0 - sigma))
         grad = grad.astype(bf16)
         grad_pre[rows, :] = grad
@@ -409,6 +398,9 @@
             grad, w_neigh[...], (((1,), (1,)), ((), ())), preferred_element_type=f32
         )
         bg[4 * gc + j] = (projected / counts).astype(bf16)
+
+    stores = [pltpu.make_async_copy(act_v, act_out, local_sem.at[6])]
+    stores[0].start()
 
     contract_rows = (((0,), (0,)), ((), ()))
     state = {}
@@ -477,7 +469,8 @@
     def sum_h():
         for copy in state["h"]:
             copy.wait_recv()
-        wfull[pl.ds(core * 256 + x * 64 + z * 16 + a * 8, 8), :] = w4[...] + rh_[...]
+        mine = pl.ds(core * 256 + x * 64 + z * 16 + a * 8, 8)
+        wfull[mine, :] = (w4[...] + rh_[...]) * (1.0 / 256.0)
         gbias_out[...] = (bias_s[3] + rb_[8])[0:1, :] * (1.0 / 256.0)
         state["gp"] = share(core * 256 + x * 64 + z * 16 + a * 8, 8, [a_peer])
 
@@ -496,15 +489,7 @@
             copy.wait_recv()
         state["gs"] = share(core * 256, 256, [sib])
 
-    def mid_gather():
-        sum_sib()
-
-    def late_gather():
-        sum_x()
-
-    def no_forward(d, other, j):
-        if j is None:
-            weight_grads()
+    def no_forward(d, other):
         return None
 
     gather(
@@ -512,17 +497,19 @@
         lambda ring, side: 4 * (ring * 2 + side),
         x,
         h,
-        x_peer[1],
-        x_peer[3],
+        x_peer,
         h_peer,
-        lambda j: bg.at[pl.ds(4 * gc + 2 * j, 2)],
+        lambda j: bg.at[pl.ds(4 * gc + j, 1)],
         no_forward,
-        (mid_gather, late_gather),
+        (weight_grads, sum_sib, sum_x),
     )
     sum_z()
 
-    multiply(4, bg, True, BWD_PAIRS)
+    prods[BWD_PAIRS] = jnp.zeros((128, 256), bf16)
+    multiply(4, bg, True, BWD_UNROLL, 0, 4)
     sum_p()
+    multiply(4, bg, True, BWD_UNROLL, 4, 8)
+    sum_h()
 
     def cols_at(d, other):
         return ((z + d) % 4) * 2 + ((1 - a) if other else a)
@@ -548,24 +535,25 @@
             mine = prods[meta[7, block_of(d, other, core) + j]].astype(f32)
             csum[shard, rows, :] = (mine + crecv[shard, rows, :].astype(f32)).astype(bf16)
 
-    def mid_scatter():
-        sum_h()
-
-    def late_scatter():
-        share_z()
-
-    scatter(bwd_bufs, csum, cols_at, z, a, z_peer, a_peer, cols_ready, (mid_scatter, late_scatter))
-    share_x()
-    gfeat_out[...] = (own_part[...] + total[...]).astype(bf16)
-    share_sib()
-    for copy in state["gs"]:
-        copy.wait_recv()
-    gself_out[...] = wfull[0:256, :] * (1.0 / 256.0)
-    gneigh_out[...] = wfull[256:512, :] * (1.0 / 256.0)
+    def weights_out():
+        for copy in state["gs"]:
+            copy.wait_recv()
+        stores.append(pltpu.make_async_copy(wfull, gweight_out, local_sem.at[7]))
+        stores[1].start()
+
+    share_z()
+    scatter(
+        bwd_bufs, csum, cols_at, z, a, z_peer, a_peer, cols_ready, (share_x, share_sib, weights_out)
+    )
+    gfeat_v[...] = (own_part[...] + total[...]).astype(bf16)
+    stores.append(pltpu.make_async_copy(gfeat_v, gfeat_out, local_sem.at[8]))
+    stores[2].start()
     net.finish()
-
-
-def layer(meta, features, tiles, w_self, w_neigh, bias, cotangent):
+    for copy in stores:
+        copy.wait()
+
+
+def layer(count, rows, cols, features, tiles, w_self, w_neigh, bias, cotangent):
     low = 512 - SPLIT_ROWS
     scatter_bufs = [
         VMEM((6, SPLIT_ROWS, 256), bf16),
@@ -576,6 +564,10 @@
         VMEM((3, low, 256), bf16),
     ]
     scratch = [
+        VMEM((8, 512), i32),
+        SMEM((8, 512), i32),
+        VMEM((512, 256), bf16),
+        VMEM((512, 256), bf16),
         VMEM((SLOTS + 1, 128, 128), bf16),
         VMEM((COL_BLOCKS, 128, 256), bf16),
         VMEM((BWD_PAIRS + 1, 128, 256), bf16),
@@ -613,7 +605,7 @@
         VMEM((512, 256), f32),
         pltpu.SemaphoreType.DMA((SEMS,)),
         pltpu.SemaphoreType.DMA((SEMS,)),
-        pltpu.SemaphoreType.DMA((5,)),
+        pltpu.SemaphoreType.DMA((9,)),
     ]
     anywhere = pl.BlockSpec(memory_space=pl.ANY)
     return pl.pallas_call(
@@ -621,26 +613,46 @@
         out_shape=(
             jax.ShapeDtypeStruct((512, 256), bf16),
             jax.ShapeDtypeStruct((512, 256), bf16),
-            jax.ShapeDtypeStruct((256, 256), f32),
-            jax.ShapeDtypeStruct((256, 256), f32),
+            jax.ShapeDtypeStruct((512, 256), f32),
             jax.ShapeDtypeStruct((1, 256), f32),
         ),
-        in_specs=[
-            pl.BlockSpec(memory_space=SMEM),
-            anywhere,
-            anywhere,
-            anywhere,
-            anywhere,
-            pl.BlockSpec(memory_space=VMEM),
-            anywhere,
-        ],
-        out_specs=[pl.BlockSpec(memory_space=VMEM)] * 5,
+        in_specs=[pl.BlockSpec(memory_space=SMEM)]
+        + [pl.BlockSpec(memory_space=VMEM)] * 2
+        + [anywhere] * 4
+        + [pl.BlockSpec(memory_space=VMEM), anywhere],
+        out_specs=[anywhere] * 3 + [pl.BlockSpec(memory_space=VMEM)],
         scratch_shapes=scratch,
         compiler_params=pltpu.CompilerParams(
             collective_id=0, has_side_effects=True, vmem_limit_bytes=60 * 1024 * 1024
         ),
         name="layer",
-    )(meta, features, tiles, w_self, w_neigh, bias, cotangent)
+    )(count, rows, cols, features, tiles, w_self, w_neigh, bias, cotangent)
+
+
+def hand_over_kernel(act, gfeat, gweight, gbias, act_out, gfeat_out, gself, gneigh, gbias_out):
+    act_out[...] = act[...]
+    gfeat_out[...] = gfeat[...]
+    gself[...] = gweight[0:256, :]
+    gneigh[...] = gweight[256:512, :]
+    gbias_out[...] = gbias[0, :]
+
+
+def hand_over(act, gfeat, gweight, gbias):
+    whole = pl.BlockSpec(memory_space=VMEM)
+    return pl.pallas_call(
+        hand_over_kernel,
+        out_shape=(
+            jax.ShapeDtypeStruct((512, 256), bf16),
+            jax.ShapeDtypeStruct((512, 256), bf16),
+            jax.ShapeDtypeStruct((256, 256), f32),
+            jax.ShapeDtypeStruct((256, 256), f32),
+            jax.ShapeDtypeStruct((256,), f32),
+        ),
+        in_specs=[whole] * 4,
+        out_specs=[whole] * 5,
+        compiler_params=pltpu.CompilerParams(vmem_limit_bytes=60 * 1024 * 1024),
+        name="hand_over",
+    )(act, gfeat, gweight, gbias)
 
 
 def local(
@@ -654,9 +666,10 @@
     bias,
     cotangent,
 ):
-    meta = plan(block_row, block_col, block_count)
-    activations, grad_features, grad_self, grad_neigh, grad_bias = layer(
-        meta,
+    results = layer(
+        block_count,
+        block_row.reshape(1, SLOTS),
+        block_col.reshape(1, SLOTS),
         features.reshape(4, 128, 256),
         block_values.reshape(SLOTS, 128, 128),
         weight_self,
@@ -664,7 +677,7 @@
         bias.reshape(1, 256),
         cotangent,
     )
-    return (activations, grad_features, grad_self, grad_neigh, grad_bias.reshape(256))
+    return hand_over(*results)
 
 
 def solution(mesh):

time: 126 us -> 109 us (0.87); the launches traced: 124 us -> 109 us
  local copies, waits for them, and re-layouts: 10.9 us -> 0 us
  Pallas kernels: 112 us -> 107 us
    unnamed x5 -> x0, local copies, waits for them, and re-layouts: 7.92 us -> none
    pallas_call x1, Pallas kernels: 109 us -> 105 us  [layer(): pl.pallas_call(layer_kernel, out_shape=(jax.ShapeDtypeStruct((512, 256),...]
    reshape x2 -> x0, local copies, waits for them, and re-layouts: 3 us -> none  [the longest x1 1.5 us: plan(): block_col.reshape(SLOTS, 1)]
where the time goes in v2:
time: 109 us
  Pallas kernels  107 us (98%)
  between operations  1.29 us (1%)
    pallas_call x1, Pallas kernels, layer(): pl.pallas_call(layer_kernel, out_shape=(jax.ShapeDtypeStruct((512, 256),...  105 us
    pallas_call x1, Pallas kernels, hand_over(): pl.pallas_call(hand_over_kernel, out_shape=(jax.ShapeDtypeStruct((512, 25...  2.19 us

profile of v2, /device:TPU:0, one launch (start us, length us, event | category | flops | bytes accessed | tf_op | source)
XLA Modules:
  0.0 108.6 jit_solution(141930993108881476)
XLA Ops:
  1.3 105.1 %layer.1 = (bf16[512,256]{1,0:T(8,128)(2,1)}, bf16[512,256]{1,0:T(8,128)(2,1)}, f32[512,256]{1,0:T(8,128)}, f32[1,256]{1,0:T(1,128)}) custom-call(s32[1,1]{1,0:T(1,128)S(6)} %copy.14.count_ref, s32[1,384]{1,0:T(1,128)} %bitcast.7, s32[1,384]{1,0:T(1,128)} %bitcast.8, bf16[4,128,256]{2,1,0:T(8,128)(2,1)} %bitcast.6, bf16[384,128,128]{2,1,0:T(8,128)(2,1)} %bitcast.5, ...), custom_call_target="tpu_custom_call" | custom-call | tf_op jit(solution)/shard_map/layer/pallas_call | solution.py:611
  106.4 2.2 %hand_over.1 = (bf16[512,256]{1,0:T(8,128)(2,1)}, bf16[512,256]{1,0:T(8,128)(2,1)}, f32[256,256]{1,0:T(8,128)}, f32[256,256]{1,0:T(8,128)}, f32[256]{0:T(256)}) custom-call(bf16[512,256]{1,0:T(8,128)(2,1)} %get-tuple-element.9.act, bf16[512,256]{1,0:T(8,128)(2,1)} %get-tuple-element.10.gfeat, f32[512,256]{1,0:T(8,128)} %get-tuple-element.11.gweight, ...), custom_call_target="tpu_custom_call" | custom-call | tf_op jit(solution)/shard_map/hand_over/pallas_call | solution.py:642

commit v3 on v2

--- a/solution.py
+++ b/solution.py
@@ -116,6 +116,7 @@
     fwd_bufs,
     bwd_bufs,
     total,
+    total_back,
     own_part,
     w_self,
     w_neigh,
@@ -123,18 +124,11 @@
     neigh,
     grad_pre,
     wg,
+    rs_,
     w1,
+    rx_,
     w2,
-    w3,
-    w4,
-    bias0,
-    bias_s,
-    rs_,
-    rx_,
     rz_,
-    rp_,
-    rh_,
-    rb_,
     wfull,
     send_sem,
     recv_sem,
@@ -158,13 +152,24 @@
     a_peer = device(a_=1 - a)
     h_peer = device(h_=1 - h)
     diagonal = {d: device(x_=(x + d) % 4, h_=1 - h) for d in (1, 2, 3)}
+    z_diagonal = {d: device(z_=(z + d) % 4, a_=1 - a) for d in (1, 2, 3)}
+    far_first = (2, 1, 3, 0)
+    row_peers = [(((x + d) % 4) * 2 + 1 - h, diagonal[d] if d else h_peer) for d in far_first]
+    row_peers += [(((x + d) % 4) * 2 + h, x_peer[d]) for d in far_first if d]
+    col_peers = [z_diagonal[d] if d else a_peer for d in far_first]
+    col_peers += [z_peer[d] for d in far_first if d]
 
     loads = [
-        pltpu.make_async_copy(tiles_hbm, tiles.at[pl.ds(0, SLOTS)], local_sem.at[0]),
-        pltpu.make_async_copy(feats, xg.at[pl.ds(4 * gr, 4)], local_sem.at[1]),
-        pltpu.make_async_copy(w_self_hbm, w_self, local_sem.at[2]),
-        pltpu.make_async_copy(w_neigh_hbm, w_neigh, local_sem.at[3]),
-        pltpu.make_async_copy(cot_hbm, cot, local_sem.at[4]),
+        pltpu.make_async_copy(
+            feats.at[:, :, pl.ds(128 * f, 128)], xg[f].at[pl.ds(4 * gr, 4)], local_sem.at[f]
+        )
+        for f in (0, 1)
+    ]
+    loads += [
+        pltpu.make_async_copy(tiles_hbm, tiles.at[pl.ds(0, SLOTS)], local_sem.at[2]),
+        pltpu.make_async_copy(w_self_hbm, w_self, local_sem.at[3]),
+        pltpu.make_async_copy(w_neigh_hbm, w_neigh, local_sem.at[4]),
+        pltpu.make_async_copy(cot_hbm, cot, local_sem.at[5]),
     ]
     for copy in loads:
         copy.start()
@@ -172,53 +177,54 @@
     barrier = pltpu.get_barrier_semaphore()
     peers = [sib, a_peer, h_peer]
     peers += list(z_peer.values()) + list(x_peer.values()) + list(diagonal.values())
+    peers += list(z_diagonal.values())
     for peer in peers:
         pl.semaphore_signal(barrier, inc=1, device_id=peer, device_id_type=MESH)
+    loads[0].wait()
+    loads[1].wait()
     pl.semaphore_wait(barrier, len(peers))
     net = Net(send_sem, recv_sem)
 
-    def gather(buf, base, ring, side, ring_peer, across, own, forward, steps):
-        def piece(d, other, j, size=1):
-            return buf.at[pl.ds(base((ring + d) % 4, (1 - side) if other else side) + j, size)]
-
+    def gather(buf, base, ring, side, ring_peer, across, forward):
         def push(d, other, j, device_id):
-            return net.put(piece(d, other, j), piece(d, other, j), device_id)
-
-        come = {}
+            at = base((ring + d) % 4, (1 - side) if other else side) + j
+            piece = buf.at[pl.ds(at, 1)]
+            return net.put(piece, piece, device_id)
+
+        near, far = {}, {}
         for j in range(4):
             for d in (2, 0, 1, 3):
-                target = ring_peer[d] if d else across
-                come[(4 - d) % 4, 0 if d else 1, j] = net.put(own(j), piece(0, 0, j), target)
-        steps[0]()
-        come[3, 0, 0].wait_recv()
-        come[3, 1, 0] = push(3, 0, 0, across)
-        come[1, 0, 0].wait_recv()
-        come[1, 1, 0] = push(1, 0, 0, across)
-        steps[1]()
+                near[(4 - d) % 4, j] = push(0, 0, j, ring_peer[d] if d else across)
+        sent = [forward(0, 0)]
+        yield
+        for d in (3, 1):
+            near[d, 0].wait_recv()
+            far[d, 0] = push(d, 0, 0, across)
+        yield
         for j in range(4):
-            come[2, 0, j].wait_recv()
-            come[2, 1, j] = push(2, 0, j, across)
+            near[2, j].wait_recv()
+            far[2, j] = push(2, 0, j, across)
             if j:
-                come[0, 1, j].wait_recv()
-                come[3, 1, j] = push(0, 1, j, ring_peer[1])
-                come[1, 1, j] = push(0, 1, j, ring_peer[3])
-        sent = [forward(0, 0), forward(2, 0)]
-        come[0, 1, 0].wait_recv()
-        sent.append(forward(0, 1))
+                near[0, j].wait_recv()
+                far[3, j] = push(0, 1, j, ring_peer[1])
+                far[1, j] = push(0, 1, j, ring_peer[3])
+        yield
+        near[0, 0].wait_recv()
         for d in (1, 3):
             for j in (1, 2, 3):
-                come[d, 0, j].wait_recv()
-            sent.append(forward(d, 0))
-        steps[2]()
+                near[d, j].wait_recv()
+        sent += [forward(0, 1), forward(1, 0), forward(3, 0), forward(2, 0)]
+        yield
         for d in (1, 3, 2):
             for j in range(4):
-                come[d, 1, j].wait_recv()
+                far[d, j].wait_recv()
             sent.append(forward(d, 1))
         for copy in sent:
             if copy is not None:
                 copy.wait_recv()
-
-    def scatter(bufs, src, at, ring, side, ring_peer, across, ready, steps):
+        yield
+
+    def scatter(bufs, src, out, at, ring, side, ring_peer, across, ready):
         ra_buf, rb_buf, r2a_src, r2a_buf, r2b_src, r2b_buf = bufs
         top, low = pl.ds(0, SPLIT_ROWS), pl.ds(SPLIT_ROWS, 512 - SPLIT_ROWS)
         near, far, far_b = {}, {}, {}
@@ -231,7 +237,7 @@
             ready(d, 0)
             if d:
                 near[d] = net.put(src.at[at(d, 0), top], ra_buf.at[2 * d - 1], ring_peer[d])
-        steps[0]()
+        yield
         second = {}
         for d in (2, 1, 3):
             far_b[d].wait_recv()
@@ -244,31 +250,34 @@
             part += ra_buf[2 * d - 2].astype(f32)
         r2a_src[...] = part.astype(bf16)
         second_a = net.put(r2a_src, r2a_buf, across)
+        yield
         part = src[at(0, 0), top].astype(f32)
         for d in (1, 3, 2):
             near[d].wait_recv()
             part += ra_buf[2 * d - 1].astype(f32)
-        total[top, :] = part
-        steps[1]()
+        out[top, :] = part
         far_b[0].wait_recv()
-        part = src[at(0, 0), low].astype(f32) + rb_buf[0].astype(f32)
-        steps[2]()
+        out[low, :] = src[at(0, 0), low].astype(f32) + rb_buf[0].astype(f32)
+        yield
         second_a.wait_recv()
-        total[top, :] += r2a_buf[...].astype(f32)
+        out[top, :] += r2a_buf[...].astype(f32)
+        part = out[low, :]
         for d in (1, 3, 2):
             second[d].wait_recv()
             part += r2b_buf[d - 1].astype(f32)
-        total[low, :] = part
-
-    def multiply(base, source, backward, unroll, begin, end):
+        out[low, :] = part
+        yield
+
+    def multiply(base, source, lanes, backward, unroll, begin, end):
         if begin == 0:
-            acc[...] = jnp.zeros_like(acc)
+            acc[:, lanes] = jnp.zeros_like(acc[:, lanes])
 
         def body(step, carry):
             for u in range(unroll):
                 p = step * unroll + u
                 left = [tiles[meta[base, 2 * p + i]] for i in (0, 1)]
-                right = jnp.concatenate([source[meta[base + 1, 2 * p + i]] for i in (0, 1)], axis=0)
+                right = [source[meta[base + 1, 2 * p + i]] for i in (0, 1)]
+                right = jnp.concatenate(right, axis=0)
                 if backward:
                     left = jnp.concatenate(left, axis=0)
                     form = (((0,), (0,)), ((), ()))
@@ -276,9 +285,9 @@
                     left = jnp.concatenate(left, axis=1)
                     form = (((1,), (0,)), ((), ()))
                 product = lax.dot_general(left, right, form, preferred_element_type=f32)
-                running = product + jnp.where(meta[base + 2, p] != 0, acc[...], 0.0)
-                acc[...] = running
-                prods[p] = running.astype(bf16)
+                running = product + jnp.where(meta[base + 2, p] != 0, acc[:, lanes], 0.0)
+                acc[:, lanes] = running
+                prods[p, :, lanes] = running.astype(bf16)
             return carry
 
         lax.fori_loop(begin, end, body, 0)
@@ -307,22 +316,16 @@
         row_s, col_s = as_column(row_l), as_column(col_l)
         meta_v[0:4, :] = order_slots(row_l, row_s, col_s, count, ROW_BLOCKS, COL_BLOCKS, FWD_PAIRS)
         meta_v[4:8, :] = order_slots(col_l, col_s, row_s, count, COL_BLOCKS, ROW_BLOCKS, BWD_PAIRS)
-        copy = pltpu.make_async_copy(meta_v, meta, local_sem.at[5])
+        copy = pltpu.make_async_copy(meta_v, meta, local_sem.at[9])
         copy.start()
         tiles[SLOTS] = jnp.zeros((128, 128), bf16)
         prods[FWD_PAIRS] = jnp.zeros((128, 256), bf16)
         degp[FWD_PAIRS] = jnp.zeros((8, 128), f32)
         copy.wait()
 
-    def count_first():
-        loads[0].wait()
-        loads[1].wait()
-        count_some(0, 4)
-
     degree_copies = []
 
     def count_last():
-        count_some(4, 8)
         degp[FWD_PAIRS] = jnp.zeros((8, 128), f32)
         sub = lax.broadcasted_iota(i32, (8, 128), 0)
         for g in range(8):
@@ -337,43 +340,80 @@
                 target = h_peer if d == 0 else (diagonal[d] if e else x_peer[d])
                 index = ((x + d) % 4) * 2 + ((1 - h) if e else h)
                 degree_copies.append(net.put(degs.at[index], degr.at[2 * d + e], target))
-        for copy in loads[2:]:
+        for copy in loads[3:]:
             copy.wait()
         for j in range(4):
+            own = jnp.concatenate([xg[f][4 * gr + j] for f in (0, 1)], axis=1)
             own_part[pl.ds(128 * j, 128), :] = (
-                jnp.dot(xg[4 * gr + j], w_self[...], preferred_element_type=f32) + bias_ref[...]
+                jnp.dot(own, w_self[...], preferred_element_type=f32) + bias_ref[...]
             )
 
-    def to_sibling(d, other):
-        at = 4 * ((1 - a if other else a) * 8 + ((z + d) % 4) * 2 + core)
-        return net.put(xg.at[pl.ds(at, 4)], xg.at[pl.ds(at, 4)], sib)
-
-    gather(
-        xg,
-        lambda ring, side: 4 * (side * 8 + ring * 2 + core),
-        z,
-        a,
-        z_peer,
-        a_peer,
-        lambda j: feats.at[pl.ds(j, 1)],
-        to_sibling,
-        (make_plan, count_first, count_last),
-    )
-
-    multiply(0, xg, False, FWD_UNROLL, 0, 8)
+    def feature_gather(f):
+        def to_sibling(d, other):
+            at = 4 * ((1 - a if other else a) * 8 + ((z + d) % 4) * 2 + core)
+            shard = xg[f].at[pl.ds(at, 4)]
+            return net.put(shard, shard, sib)
+
+        return gather(
+            xg[f],
+            lambda ring, side: 4 * (side * 8 + ring * 2 + core),
+            z,
+            a,
+            z_peer,
+            a_peer,
+            to_sibling,
+        )
 
     def rows_at(d, other):
         return ((x + d) % 4) * 2 + ((1 - h) if other else h)
 
-    def rows_ready(d, other):
-        shard = rows_at(d, other)
-        for j in range(4):
-            rowsum[shard, pl.ds(128 * j, 128), :] = prods[meta[3, 4 * shard + j]]
-
-    def nothing():
-        pass
-
-    scatter(fwd_bufs, rowsum, rows_at, x, h, x_peer, h_peer, rows_ready, (nothing,) * 3)
+    def row_scatter(f):
+        def rows_ready(d, other):
+            shard = rows_at(d, other)
+            for j in range(4):
+                rowsum[f, shard, pl.ds(128 * j, 128), :] = prods[
+                    meta[3, 4 * shard + j], :, pl.ds(128 * f, 128)
+                ]
+
+        bufs = [buf.at[f] for buf in fwd_bufs]
+        return scatter(
+            bufs, rowsum.at[f], total.at[f], rows_at, x, h, x_peer, h_peer, rows_ready
+        )
+
+    def forward_part(f, begin, end):
+        multiply(0, xg[f], pl.ds(128 * f, 128), False, FWD_UNROLL, begin, end)
+
+    get = [feature_gather(0), feature_gather(1)]
+    put = [row_scatter(0), row_scatter(1)]
+    next(get[0])
+    make_plan()
+    loads[2].wait()
+    next(get[0])
+    count_some(0, 2)
+    next(get[0])
+    next(get[1])
+    count_some(2, 6)
+    next(get[0])
+    count_some(6, 8)
+    count_last()
+    next(get[0])
+    forward_part(0, 0, 2)
+    next(get[1])
+    forward_part(0, 2, 4)
+    next(get[1])
+    forward_part(0, 4, 6)
+    next(get[1])
+    forward_part(0, 6, 8)
+    next(put[0])
+    next(get[1])
+    forward_part(1, 0, 8)
+    next(put[0])
+    next(put[1])
+    next(put[0])
+    next(put[1])
+    next(put[0])
+    next(put[1])
+    next(put[1])
 
     degree = degs[gc]
     for copy in degree_copies:
@@ -386,7 +426,8 @@
         rows = pl.ds(128 * j, 128)
         counts = jnp.broadcast_to(degree[j : j + 1, :], (128, 128)).T
         counts = jnp.concatenate([counts, counts], axis=1)
-        mean = (total[rows, :] / counts).astype(bf16)
+        summed = jnp.concatenate([total[f, rows, :] for f in (0, 1)], axis=1)
+        mean = (summed / counts).astype(bf16)
         neigh[rows, :] = mean
         preact = own_part[rows, :] + jnp.dot(mean, w_neigh[...], preferred_element_type=f32)
         sigma = jax.nn.sigmoid(preact)
@@ -406,19 +447,19 @@
     state = {}
 
     def weight_grads():
-        own = jnp.concatenate([xg[4 * gr + j] for j in range(4)], axis=0)
         grad = grad_pre[...]
-        wg[0:256, :] = lax.dot_general(own, grad, contract_rows, preferred_element_type=f32)
-        wg[256:512, :] = lax.dot_general(
+        for f in (0, 1):
+            own = jnp.concatenate([xg[f][4 * gr + j] for j in range(4)], axis=0)
+            wg[0, pl.ds(128 * f, 128), :] = lax.dot_general(
+                own, grad, contract_rows, preferred_element_type=f32
+            )
+        wg[1, 0:256, :] = lax.dot_general(
             neigh[...], grad, contract_rows, preferred_element_type=f32
         )
-        bias0[...] = jnp.broadcast_to(
-            jnp.sum(grad.astype(f32), axis=0, keepdims=True), (8, 256)
-        )
-        state["s"] = [
-            net.put(wg.at[pl.ds((1 - core) * 256, 256)], rs_, sib),
-            net.put(bias0, rb_.at[0], sib),
-        ]
+        bias = jnp.sum(grad.astype(f32), axis=0, keepdims=True)
+        for side in (0, 1):
+            wg[side, 256:264, :] = jnp.broadcast_to(bias, (8, 256))
+        state["s"] = [net.put(wg.at[1 - core], rs_, sib)]
         own_part[...] = lax.dot_general(
             grad, w_self[...], (((1,), (1,)), ((), ())), preferred_element_type=f32
         )
@@ -426,91 +467,44 @@
     def sum_sib():
         for copy in state["s"]:
             copy.wait_recv()
-        w1[...] = wg[pl.ds(core * 256, 256), :] + rs_[...]
-        bias_s[0] = bias0[...] + rb_[0]
-        state["x"] = []
-        for d in (2, 1, 3):
-            src = w1.at[pl.ds(((x + d) % 4) * 64, 64)]
-            state["x"].append(net.put(src, rx_.at[d - 1], x_peer[d]))
-            state["x"].append(net.put(bias_s.at[0], rb_.at[d], x_peer[d]))
-
-    def sum_x():
+        both = wg[core] + rs_[...]
+        for g in range(8):
+            w1[g, 0:32, :] = both[32 * g : 32 * g + 32, :]
+            w1[g, 32:40, :] = both[256:264, :]
+        rx_[gc] = w1[gc]
+        state["x"] = [net.put(w1.at[to], rx_.at[gc], target) for to, target in row_peers]
+
+    def sum_row():
         for copy in state["x"]:
             copy.wait_recv()
-        w2[...] = w1[pl.ds(x * 64, 64), :] + rx_[0] + rx_[1] + rx_[2]
-        bias_s[1] = bias_s[0] + rb_[1] + rb_[2] + rb_[3]
-        state["z"] = []
-        for d in (2, 1, 3):
-            src = w2.at[pl.ds(((z + d) % 4) * 16, 16)]
-            state["z"].append(net.put(src, rz_.at[d - 1], z_peer[d]))
-            state["z"].append(net.put(bias_s.at[1], rb_.at[3 + d], z_peer[d]))
-
-    def sum_z():
+        part = rx_[0]
+        for g in range(1, 8):
+            part += rx_[g]
+        w2[...] = part
+        rz_[z * 2 + a] = part
+        state["z"] = [net.put(w2, rz_.at[z * 2 + a], target) for target in col_peers]
+
+    def sum_all():
         for copy in state["z"]:
             copy.wait_recv()
-        w3[...] = w2[pl.ds(z * 16, 16), :] + rz_[0] + rz_[1] + rz_[2]
-        bias_s[2] = bias_s[1] + rb_[4] + rb_[5] + rb_[6]
-        state["p"] = [
-            net.put(w3.at[pl.ds((1 - a) * 8, 8)], rp_, a_peer),
-            net.put(bias_s.at[2], rb_.at[7], a_peer),
-        ]
-
-    def sum_p():
-        for copy in state["p"]:
-            copy.wait_recv()
-        w4[...] = w3[pl.ds(a * 8, 8), :] + rp_[...]
-        bias_s[3] = bias_s[2] + rb_[7]
-        state["h"] = [net.put(w4, rh_, h_peer), net.put(bias_s.at[3], rb_.at[8], h_peer)]
-
-    def share(rows, size, targets):
-        part = wfull.at[pl.ds(rows, size)]
-        return [net.put(part, part, target) for target in targets]
-
-    def sum_h():
-        for copy in state["h"]:
-            copy.wait_recv()
-        mine = pl.ds(core * 256 + x * 64 + z * 16 + a * 8, 8)
-        wfull[mine, :] = (w4[...] + rh_[...]) * (1.0 / 256.0)
-        gbias_out[...] = (bias_s[3] + rb_[8])[0:1, :] * (1.0 / 256.0)
-        state["gp"] = share(core * 256 + x * 64 + z * 16 + a * 8, 8, [a_peer])
-
-    def share_z():
-        for copy in state["gp"]:
-            copy.wait_recv()
-        state["gz"] = share(core * 256 + x * 64 + z * 16, 16, list(z_peer.values()))
-
-    def share_x():
-        for copy in state["gz"]:
-            copy.wait_recv()
-        state["gx"] = share(core * 256 + x * 64, 64, list(x_peer.values()))
+        part = rz_[0]
+        for g in range(1, 8):
+            part += rz_[g]
+        mine = pl.ds(core * 256 + gc * 32, 32)
+        wfull[mine, :] = part[0:32, :] * (1.0 / 256.0)
+        gbias_out[...] = part[32:33, :] * (1.0 / 256.0)
+        piece = wfull.at[mine]
+        state["gx"] = [net.put(piece, piece, target) for _, target in row_peers]
 
     def share_sib():
         for copy in state["gx"]:
             copy.wait_recv()
-        state["gs"] = share(core * 256, 256, [sib])
+        half = wfull.at[pl.ds(core * 256, 256)]
+        state["gs"] = [net.put(half, half, sib)]
 
     def no_forward(d, other):
         return None
 
-    gather(
-        bg,
-        lambda ring, side: 4 * (ring * 2 + side),
-        x,
-        h,
-        x_peer,
-        h_peer,
-        lambda j: bg.at[pl.ds(4 * gc + j, 1)],
-        no_forward,
-        (weight_grads, sum_sib, sum_x),
-    )
-    sum_z()
-
-    prods[BWD_PAIRS] = jnp.zeros((128, 256), bf16)
-    multiply(4, bg, True, BWD_UNROLL, 0, 4)
-    sum_p()
-    multiply(4, bg, True, BWD_UNROLL, 4, 8)
-    sum_h()
-
     def cols_at(d, other):
         return ((z + d) % 4) * 2 + ((1 - a) if other else a)
 
@@ -518,14 +512,16 @@
         return 4 * (((1 - a) if other else a) * 8 + ((z + d) % 4) * 2 + core_)
 
     to_sib = {}
-    for other in (1, 0):
-        for d in (2, 1, 3, 0):
-            shard = cols_at(d, other)
-            for j in range(4):
-                csend[shard, pl.ds(128 * j, 128), :] = prods[
-                    meta[7, block_of(d, other, 1 - core) + j]
-                ]
-            to_sib[d, other] = net.put(csend.at[shard], crecv.at[shard], sib)
+
+    def cols_to_sibling():
+        for other in (1, 0):
+            for d in (2, 1, 3, 0):
+                shard = cols_at(d, other)
+                for j in range(4):
+                    csend[shard, pl.ds(128 * j, 128), :] = prods[
+                        meta[7, block_of(d, other, 1 - core) + j]
+                    ]
+                to_sib[d, other] = net.put(csend.at[shard], crecv.at[shard], sib)
 
     def cols_ready(d, other):
         shard = cols_at(d, other)
@@ -541,11 +537,29 @@
         stores.append(pltpu.make_async_copy(wfull, gweight_out, local_sem.at[7]))
         stores[1].start()
 
-    share_z()
-    scatter(
-        bwd_bufs, csum, cols_at, z, a, z_peer, a_peer, cols_ready, (share_x, share_sib, weights_out)
-    )
-    gfeat_v[...] = (own_part[...] + total[...]).astype(bf16)
+    get = gather(bg, lambda ring, side: 4 * (ring * 2 + side), x, h, x_peer, h_peer, no_forward)
+    put = scatter(bwd_bufs, csum, total_back, cols_at, z, a, z_peer, a_peer, cols_ready)
+    every = pl.ds(0, 256)
+    next(get)
+    next(get)
+    next(get)
+    weight_grads()
+    next(get)
+    next(get)
+    sum_sib()
+    prods[BWD_PAIRS] = jnp.zeros((128, 256), bf16)
+    multiply(4, bg, every, True, BWD_UNROLL, 0, 4)
+    sum_row()
+    multiply(4, bg, every, True, BWD_UNROLL, 4, 8)
+    cols_to_sibling()
+    sum_all()
+    next(put)
+    next(put)
+    share_sib()
+    next(put)
+    weights_out()
+    next(put)
+    gfeat_v[...] = (own_part[...] + total_back[...]).astype(bf16)
     stores.append(pltpu.make_async_copy(gfeat_v, gfeat_out, local_sem.at[8]))
     stores[2].start()
     net.finish()
@@ -555,33 +569,36 @@
 
 def layer(count, rows, cols, features, tiles, w_self, w_neigh, bias, cotangent):
     low = 512 - SPLIT_ROWS
-    scatter_bufs = [
-        VMEM((6, SPLIT_ROWS, 256), bf16),
-        VMEM((4, low, 256), bf16),
-        VMEM((SPLIT_ROWS, 256), bf16),
-        VMEM((SPLIT_ROWS, 256), bf16),
-        VMEM((3, low, 256), bf16),
-        VMEM((3, low, 256), bf16),
-    ]
+    def scatter_bufs(*lead, width):
+        return [
+            VMEM((*lead, 6, SPLIT_ROWS, width), bf16),
+            VMEM((*lead, 4, low, width), bf16),
+            VMEM((*lead, SPLIT_ROWS, width), bf16),
+            VMEM((*lead, SPLIT_ROWS, width), bf16),
+            VMEM((*lead, 3, low, width), bf16),
+            VMEM((*lead, 3, low, width), bf16),
+        ]
+
     scratch = [
         VMEM((8, 512), i32),
         SMEM((8, 512), i32),
         VMEM((512, 256), bf16),
         VMEM((512, 256), bf16),
         VMEM((SLOTS + 1, 128, 128), bf16),
-        VMEM((COL_BLOCKS, 128, 256), bf16),
+        [VMEM((COL_BLOCKS, 128, 128), bf16)] * 2,
         VMEM((BWD_PAIRS + 1, 128, 256), bf16),
         VMEM((128, 256), f32),
         VMEM((FWD_PAIRS + 1, 8, 128), f32),
         VMEM((8, 8, 128), f32),
         VMEM((8, 8, 128), f32),
-        VMEM((8, 512, 256), bf16),
+        VMEM((2, 8, 512, 128), bf16),
         VMEM((ROW_BLOCKS, 128, 256), bf16),
         VMEM((8, 512, 256), bf16),
         VMEM((8, 512, 256), bf16),
         VMEM((8, 512, 256), bf16),
-        scatter_bufs,
-        scatter_bufs,
+        scatter_bufs(2, width=128),
+        scatter_bufs(width=256),
+        VMEM((2, 512, 128), f32),
         VMEM((512, 256), f32),
         VMEM((512, 256), f32),
         VMEM((256, 256), bf16),
@@ -589,23 +606,16 @@
         VMEM((512, 256), bf16),
         VMEM((512, 256), bf16),
         VMEM((512, 256), bf16),
-        VMEM((512, 256), f32),
-        VMEM((256, 256), f32),
-        VMEM((64, 256), f32),
-        VMEM((16, 256), f32),
-        VMEM((8, 256), f32),
-        VMEM((8, 256), f32),
-        VMEM((4, 8, 256), f32),
-        VMEM((256, 256), f32),
-        VMEM((3, 64, 256), f32),
-        VMEM((3, 16, 256), f32),
-        VMEM((8, 256), f32),
-        VMEM((8, 256), f32),
-        VMEM((9, 8, 256), f32),
+        VMEM((2, 264, 256), f32),
+        VMEM((264, 256), f32),
+        VMEM((8, 40, 256), f32),
+        VMEM((8, 40, 256), f32),
+        VMEM((40, 256), f32),
+        VMEM((8, 40, 256), f32),
         VMEM((512, 256), f32),
         pltpu.SemaphoreType.DMA((SEMS,)),
         pltpu.SemaphoreType.DMA((SEMS,)),
-        pltpu.SemaphoreType.DMA((9,)),
+        pltpu.SemaphoreType.DMA((10,)),
     ]
     anywhere = pl.BlockSpec(memory_space=pl.ANY)
     return pl.pallas_call(

time: 109 us -> 105 us (0.963)
  Pallas kernels: 107 us -> 103 us
    pallas_call x1, Pallas kernels: 105 us -> 101 us  [layer(): pl.pallas_call(layer_kernel, out_shape=(jax.ShapeDtypeStruct((512, 256),...]
where the time goes in v3:
time: 105 us
  Pallas kernels  103 us (98%)
  between operations  1.29 us (1%)
    pallas_call x1, Pallas kernels, layer(): pl.pallas_call(layer_kernel, out_shape=(jax.ShapeDtypeStruct((512, 256),...  101 us
    pallas_call x1, Pallas kernels, hand_over(): pl.pallas_call(hand_over_kernel, out_shape=(jax.ShapeDtypeStruct((512, 25...  2.19 us

profile of v3, /device:TPU:0, one launch (start us, length us, event | category | flops | bytes accessed | tf_op | source)
XLA Modules:
  0.0 104.6 jit_solution(2938182085477220622)
XLA Ops:
  1.3 101.1 %layer.1 = (bf16[512,256]{1,0:T(8,128)(2,1)}, bf16[512,256]{1,0:T(8,128)(2,1)}, f32[512,256]{1,0:T(8,128)}, f32[1,256]{1,0:T(1,128)}) custom-call(s32[1,1]{1,0:T(1,128)S(6)} %copy.14.count_ref, s32[1,384]{1,0:T(1,128)} %bitcast.7, s32[1,384]{1,0:T(1,128)} %bitcast.8, bf16[4,128,256]{2,1,0:T(8,128)(2,1)} %bitcast.6, bf16[384,128,128]{2,1,0:T(8,128)(2,1)} %bitcast.5, ...), custom_call_target="tpu_custom_call" | custom-call | tf_op jit(solution)/shard_map/layer/pallas_call | solution.py:621
  102.4 2.2 %hand_over.1 = (bf16[512,256]{1,0:T(8,128)(2,1)}, bf16[512,256]{1,0:T(8,128)(2,1)}, f32[256,256]{1,0:T(8,128)}, f32[256,256]{1,0:T(8,128)}, f32[256]{0:T(256)}) custom-call(bf16[512,256]{1,0:T(8,128)(2,1)} %get-tuple-element.9.act, bf16[512,256]{1,0:T(8,128)(2,1)} %get-tuple-element.10.gfeat, f32[512,256]{1,0:T(8,128)} %get-tuple-element.11.gweight, ...), custom_call_target="tpu_custom_call" | custom-call | tf_op jit(solution)/shard_map/hand_over/pallas_call | solution.py:652

commit v4 on v3

--- a/solution.py
+++ b/solution.py
@@ -185,7 +185,7 @@
     pl.semaphore_wait(barrier, len(peers))
     net = Net(send_sem, recv_sem)
 
-    def gather(buf, base, ring, side, ring_peer, across, forward):
+    def gather(buf, base, ring, side, ring_peer, across, forward, make=None):
         def push(d, other, j, device_id):
             at = base((ring + d) % 4, (1 - side) if other else side) + j
             piece = buf.at[pl.ds(at, 1)]
@@ -193,6 +193,8 @@
 
         near, far = {}, {}
         for j in range(4):
+            if make is not None:
+                make(j)
             for d in (2, 0, 1, 3):
                 near[(4 - d) % 4, j] = push(0, 0, j, ring_peer[d] if d else across)
         sent = [forward(0, 0)]
@@ -311,7 +313,7 @@
         lax.fori_loop(begin, end, body, 0)
 
     def make_plan():
-        count = count_ref[0, 0]
+        count = count_ref[...]
         row_l, col_l = row_ref[...], col_ref[...]
         row_s, col_s = as_column(row_l), as_column(col_l)
         meta_v[0:4, :] = order_slots(row_l, row_s, col_s, count, ROW_BLOCKS, COL_BLOCKS, FWD_PAIRS)
@@ -421,8 +423,7 @@
     for slot in range(1, 8):
         degree += degr[slot]
     degree = jnp.maximum(degree, 1.0)
-    gathered = {}
-    for j in range(4):
+    def dense_block(j):
         rows = pl.ds(128 * j, 128)
         counts = jnp.broadcast_to(degree[j : j + 1, :], (128, 128)).T
         counts = jnp.concatenate([counts, counts], axis=1)
@@ -440,8 +441,6 @@
         )
         bg[4 * gc + j] = (projected / counts).astype(bf16)
 
-    stores = [pltpu.make_async_copy(act_v, act_out, local_sem.at[6])]
-    stores[0].start()
 
     contract_rows = (((0,), (0,)), ((), ()))
     state = {}
@@ -537,10 +536,12 @@
         stores.append(pltpu.make_async_copy(wfull, gweight_out, local_sem.at[7]))
         stores[1].start()
 
-    get = gather(bg, lambda ring, side: 4 * (ring * 2 + side), x, h, x_peer, h_peer, no_forward)
+    get = gather(bg, lambda ring, side: 4 * (ring * 2 + side), x, h, x_peer, h_peer, no_forward, dense_block)
     put = scatter(bwd_bufs, csum, total_back, cols_at, z, a, z_peer, a_peer, cols_ready)
     every = pl.ds(0, 256)
     next(get)
+    stores = [pltpu.make_async_copy(act_v, act_out, local_sem.at[6])]
+    stores[0].start()
     next(get)
     next(get)
     weight_grads()
@@ -626,8 +627,7 @@
             jax.ShapeDtypeStruct((512, 256), f32),
             jax.ShapeDtypeStruct((1, 256), f32),
         ),
-        in_specs=[pl.BlockSpec(memory_space=SMEM)]
-        + [pl.BlockSpec(memory_space=VMEM)] * 2
+        in_specs=[pl.BlockSpec(memory_space=VMEM)] * 3
         + [anywhere] * 4
         + [pl.BlockSpec(memory_space=VMEM), anywhere],
         out_specs=[anywhere] * 3 + [pl.BlockSpec(memory_space=VMEM)],

time: 105 us -> 104 us (level)
  no operation moved by 1% of the time
where the time goes in v4:
time: 104 us
  Pallas kernels  103 us (99%)
  between operations  1.29 us (1%)
    pallas_call x1, Pallas kernels, layer(): pl.pallas_call(layer_kernel, out_shape=(jax.ShapeDtypeStruct((512, 256),...  101 us
    pallas_call x1, Pallas kernels, hand_over(): pl.pallas_call(hand_over_kernel, out_shape=(jax.ShapeDtypeStruct((512, 25...  2.19 us

profile of v4, /device:TPU:0, one launch (start us, length us, event | category | flops | bytes accessed | tf_op | source)
XLA Modules:
  0.0 104.3 jit_solution(6167911228896326133)
XLA Ops:
  1.3 100.8 %layer.1 = (bf16[512,256]{1,0:T(8,128)(2,1)}, bf16[512,256]{1,0:T(8,128)(2,1)}, f32[512,256]{1,0:T(8,128)}, f32[1,256]{1,0:T(1,128)}) custom-call(s32[1,1]{1,0:T(1,128)S(6)} %copy.14.count_ref, s32[1,384]{1,0:T(1,128)} %bitcast.7, s32[1,384]{1,0:T(1,128)} %bitcast.8, bf16[4,128,256]{2,1,0:T(8,128)(2,1)} %bitcast.6, bf16[384,128,128]{2,1,0:T(8,128)(2,1)} %bitcast.5, ...), custom_call_target="tpu_custom_call" | custom-call | tf_op jit(solution)/shard_map/layer/pallas_call | solution.py:622
  102.1 2.2 %hand_over.1 = (bf16[512,256]{1,0:T(8,128)(2,1)}, bf16[512,256]{1,0:T(8,128)(2,1)}, f32[256,256]{1,0:T(8,128)}, f32[256,256]{1,0:T(8,128)}, f32[256]{0:T(256)}) custom-call(bf16[512,256]{1,0:T(8,128)(2,1)} %get-tuple-element.9.act, bf16[512,256]{1,0:T(8,128)(2,1)} %get-tuple-element.10.gfeat, f32[512,256]{1,0:T(8,128)} %get-tuple-element.11.gweight, ...), custom_call_target="tpu_custom_call" | custom-call | tf_op jit(solution)/shard_map/hand_over/pallas_call | solution.py:652
